TPU v7x, 32 devices: a whole 2x2x4 slice. The times are simulated.
32 devices in a mesh: clips: 2 (over y), tm: 4 (over x, core), rows: 4 (over z).
Axes of the slice: x: 2, y: 2, z: 4, core: 2. Of those that a mesh axis runs over, the one named last changes fastest.
Arguments:
- segment_input: bfloat16 [4, 8, 4, 32, 384], P('clips', 'tm', 'rows'), parts along dimension 0, may hold values from -6 to 6
- inner_input: bfloat16 [4, 8, 4, 32, 384], P('clips', 'tm', 'rows'), parts along dimension 0, may hold values from -6 to 6
- lengths: int32 [4, 4], P('clips', 'tm'), parts along dimension 0, may hold values from 1 to 2
- inner_gain: float32 [384], replicated, may hold values from 0.25 to 1.75
- causal_weight: bfloat16 [3, 3, 3, 384, 384], replicated, may hold values from -0.0625 to 0.0625
- causal_bias: float32 [384], replicated, may hold values from -3 to 3
- attention_gain: float32 [384], replicated, may hold values from 0.25 to 1.75
- triple_weight: bfloat16 [384, 1152], replicated, may hold values from -0.4375 to 0.4375
- triple_bias: float32 [1152], replicated, may hold values from -150 to 150
- output_weight: bfloat16 [384, 384], replicated, may hold values from -0.3125 to 0.3125
- output_bias: float32 [384], replicated, may hold values from -3 to 3
Outputs:
- encoded: bfloat16 [4, 8, 4, 32, 384], P('clips', 'tm', 'rows'), parts along dimension 0
There are 2 independent parts, one for each index of `clips`. A program takes and returns all parts, laid end to end along the dimension named above; an argument that names none is the same for every part. Nothing has to cross between parts.
Inputs may be any that keep to these rules, and one draw needn't show every extreme that they name: The valid frames of a clip in a section are that section's first lengths[b, s] frame slots.
All inputs are finite; a program needn't handle non-finite values.
Results may differ from a plain program's by a relative error of at most 0.0062.
Values may be sent and summed in bfloat16 or wider, within the bound.
A program may use at most 128 MiB of HBM per device.

v0:
```python
import math

import jax
import jax.numpy as jnp
from jax import lax
from jax.sharding import PartitionSpec as P

EPSILON = 1e-06


def prefix(part, axis, combine, identity):
    place = lax.axis_index(axis)
    gathered = jax.tree.map(lambda a: lax.all_gather(a, axis), part)
    state = jax.tree.map(lambda a, e: jnp.zeros_like(a) + jnp.asarray(e, a.dtype), part, identity)

    def one(step, state):
        return combine(
            state, jax.tree.map(lambda a: lax.dynamic_index_in_dim(a, step, 0, False), gathered)
        )

    return lax.fori_loop(0, place, one, state)


def as_sent(x):

    def short(part):
        return part.astype(jnp.bfloat16) if part.dtype == jnp.float32 else part

    return jax.tree.map(short, x)


def with_halo(cells, sides, width):
    for axis, dim in sides:
        count = lax.axis_size(axis)
        ends = count - 1
        head = lax.slice_in_dim(cells, 0, width, axis=dim)
        tail = lax.slice_in_dim(cells, cells.shape[dim] - width, cells.shape[dim], axis=dim)
        cells = jnp.concatenate(
            [
                lax.ppermute(tail, axis, [(i, (i + 1) % count) for i in range(ends)]),
                cells,
                lax.ppermute(head, axis, [((i + 1) % count, i) for i in range(ends)]),
            ],
            axis=dim,
        )
    return cells


def normalize(field, gain):
    widened = field.astype(jnp.float32)
    return widened * lax.rsqrt(jnp.mean(widened * widened, axis=-1, keepdims=True) + EPSILON) * gain


def last_two(extended, counts):
    slot_total = extended.shape[1]
    chosen = []
    for position in range(2):
        target = counts + position
        picked = jnp.zeros_like(extended[:, 0])
        for slot_index in range(slot_total):
            matches = (target == slot_index)[:, None, None, None]
            picked = jnp.where(matches, extended[:, slot_index], picked)
        chosen.append(picked)
    return jnp.stack(chosen, axis=1)


def summarize(activated, counts):
    blanks = jnp.zeros((activated.shape[0], 2) + activated.shape[2:], activated.dtype)
    summary = last_two(jnp.concatenate([blanks, activated], axis=1), counts)
    return (summary, jnp.minimum(counts, 2).astype(jnp.bfloat16))


def join_later(earlier, later):
    early_frames, early_count = earlier
    late_frames, late_count = later
    complete = (late_count > 1.5)[:, None, None, None, None]
    single = (late_count > 0.5)[:, None, None, None, None]
    shifted = jnp.concatenate([early_frames[:, 1:], late_frames[:, 1:]], axis=1)
    frames = jnp.where(complete, late_frames, jnp.where(single, shifted, early_frames))
    total_count = jnp.minimum(early_count + late_count, 2.0).astype(early_count.dtype)
    return (frames, total_count)


def incoming_cache(summary, counts):
    starting = (jnp.zeros_like(summary), jnp.zeros_like(counts))
    combined = prefix((summary, counts), "tm", join_later, starting)
    return combined[0]


def convolve(padded, causal_weight, causal_bias):
    clip_count, slot_total, rows_padded, column_count, channels = padded.shape
    frame_count = slot_total - 2
    row_count = rows_padded - 2
    widened = jnp.pad(padded, ((0, 0), (0, 0), (0, 0), (1, 1), (0, 0)))
    summed = jnp.zeros((clip_count * frame_count * row_count * column_count, channels), jnp.float32)
    for delta_time in range(3):
        for delta_row in range(3):
            window = widened[
                :, delta_time : delta_time + frame_count, delta_row : delta_row + row_count
            ]
            columns = jnp.concatenate(
                [window[:, :, :, delta_col : delta_col + column_count] for delta_col in range(3)],
                axis=-1,
            )
            kernel = causal_weight[delta_time, delta_row].reshape(3 * channels, channels)
            summed = summed + jnp.dot(
                columns.reshape(-1, 3 * channels), kernel, preferred_element_type=jnp.float32
            )
    return summed.reshape(clip_count, frame_count, row_count, column_count, channels) + causal_bias


def attend(normed, triple_weight, triple_bias, output_weight, output_bias):
    frame_count, places, channels = normed.shape
    packed = (
        jnp.dot(normed.reshape(-1, channels), triple_weight, preferred_element_type=jnp.float32)
        + triple_bias
    )
    packed = packed.reshape(frame_count, places, 3 * channels)
    queries = packed[:, :, :channels]
    key_vectors = packed[:, :, channels : 2 * channels]
    values = packed[:, :, 2 * channels :].astype(jnp.bfloat16)
    scores = jnp.einsum(
        "nqc,nkc->nqk", queries, key_vectors, precision=lax.Precision.HIGHEST
    ) / math.sqrt(channels)
    row_max = jnp.max(scores, axis=-1, keepdims=True)
    exponent = jnp.exp(scores - row_max)
    weights = (exponent / jnp.sum(exponent, axis=-1, keepdims=True)).astype(jnp.bfloat16)
    attended = jnp.einsum(
        "nqk,nkc->nqc", weights, values, preferred_element_type=jnp.float32
    ).astype(jnp.bfloat16)
    projected = (
        jnp.dot(attended.reshape(-1, channels), output_weight, preferred_element_type=jnp.float32)
        + output_bias
    )
    return projected.reshape(frame_count, places, channels).astype(jnp.bfloat16)


def body(
    segment_input,
    inner_input,
    lengths,
    inner_gain,
    causal_weight,
    causal_bias,
    attention_gain,
    triple_weight,
    triple_bias,
    output_weight,
    output_bias,
):
    clip_count, frame_count, row_count, column_count, channels = segment_input.shape
    activated = jax.nn.silu(normalize(inner_input, inner_gain)).astype(jnp.bfloat16)
    counts = lengths[:, 0]
    live_mask = (jnp.arange(frame_count, dtype=jnp.int32)[None, :] < counts[:, None]).astype(
        jnp.float32
    )
    carried = incoming_cache(*summarize(activated, counts))
    extended = jnp.concatenate([carried, activated], axis=1)
    padded = with_halo(as_sent(extended), (("rows", 2),), 1).astype(extended.dtype)
    convolved = convolve(padded, causal_weight, causal_bias)
    residual = (segment_input.astype(jnp.float32) + convolved).astype(jnp.bfloat16)
    residual = lax.optimization_barrier(residual)
    normed = normalize(residual, attention_gain).astype(jnp.bfloat16)
    row_devices = lax.axis_size("rows")
    per_device = clip_count * frame_count // row_devices
    grouped = normed.reshape(row_devices, per_device, row_count, column_count, channels)
    portion = lax.all_to_all(grouped, "rows", split_axis=0, concat_axis=2, tiled=True)
    owned = portion.shape[1]
    height = portion.shape[2]
    flat = portion.reshape(owned, height * column_count, channels)
    result = attend(flat, triple_weight, triple_bias, output_weight, output_bias)
    result = result.reshape(1, owned, height, column_count, channels)
    projected = lax.all_to_all(result, "rows", split_axis=2, concat_axis=0, tiled=True)
    projected = projected.reshape(clip_count, frame_count, row_count, column_count, channels)
    projected = lax.optimization_barrier(projected)
    summed = residual.astype(jnp.float32) + projected.astype(jnp.float32)
    return (summed * live_mask[:, :, None, None, None]).astype(jnp.bfloat16)


def solution(mesh):
    placed = (
        P("clips", "tm", "rows", None, None),
        P("clips", "tm", "rows", None, None),
        P("clips", "tm"),
        P(),
        P(),
        P(),
        P(),
        P(),
        P(),
        P(),
        P(),
    )
    return jax.shard_map(
        body,
        mesh=mesh,
        in_specs=placed,
        out_specs=P("clips", "tm", "rows", None, None),
        check_vma=False,
    )
```

profile of v0, /device:TPU:0, one launch (start us, length us, event | category | flops | bytes accessed | tf_op | source)
XLA Modules:
  0.0 58.6 jit_solution(12638604743484779682)
XLA Ops:
  0.0 0.7 %convert_bitcast_fusion = bf16[2]{0:T(256)(128)(2,1)S(1)} fusion(s32[2,1]{0,1:T(1,128)} %param.15), kind=kLoop, calls=%fused_computation.75 | loop fusion | flops 4 | bytes 12
  0.7 0.7 %broadcast_compare_fusion.1 = (pred[2]{0:T(512)(128)(4,1)S(1)}, pred[2]{0:T(512)(128)(4,1)S(1)}, pred[2]{0:T(512)(128)(4,1)S(1)}, pred[2]{0:T(512)(128)(4,1)S(1)}) fusion(s32[2,1]{0,1:T(1,128)} %param.15), kind=kLoop, calls=%fused_computation.79 | loop fusion | flops 10 | bytes 16 | tf_op jit(solution)/shard_map/eq | solution.py:61
  1.4 1.0 %fusion.7 = f32[2,2,32]{2,1,0:T(2,128)S(1)} fusion(bf16[2,2,1,32,384]{4,3,2,1,0:T(8,128)(2,1)} %param.14), kind=kLoop, calls=%fused_computation.45 | loop fusion | flops 147328 | bytes 98816 | tf_op jit(solution)/shard_map/reduce_sum | solution.py:51
  2.4 1.3 %dynamic-slice = u32[1]{0:T(128)} dynamic-slice(u32[32]{0:T(128)} %constant.64, u32[]{:T(128)S(6)} %add.130), dynamic_slice_sizes={1} | dynamic-slice | bytes 12
  4.6 8.3 %all-reduce.1 = bf16[8]{0:T(256)(128)(2,1)S(1)} all-reduce(bf16[8]{0:T(256)(128)(2,1)S(1)} %dynamic-update-slice), channel_id=2, replica_groups=mesh['clips'=2,'tm'=4,'rows'=4] {'tm'}, use_global_device_ids=true, to_apply=%add.1 | all-reduce | flops 8 | bytes 32
  13.0 1.0 %fusion.14 = bf16[2,2,1,32,384]{4,3,2,1,0:T(8,128)(2,1)S(1)} fusion(bf16[2,2,1,32,384]{4,3,2,1,0:T(8,128)(2,1)} %param.14, f32[384]{0:T(512)} %param.16, f32[2,2,32]{2,1,0:T(2,128)S(1)} %add_rsqrt_fusion.1), kind=kLoop, calls=%fused_computation.52 | loop fusion | flops 393216 | bytes 198656 | tf_op jit(solution)/shard_map/convert_element_type | solution.py:152
  14.1 6.1 %all-gather.1 = bf16[8,2,1,32,384]{4,3,2,1,0:T(8,128)(2,1)S(1)} all-gather(bf16[2,2,1,32,384]{4,3,2,1,0:T(8,128)(2,1)S(1)} %pad_maximum_fusion.10), channel_id=3, replica_groups=mesh['clips'=2,'tm'=4,'rows'=4] {'tm'}, dimensions={0}, use_global_device_ids=true | all-gather | bytes 491520 | tf_op jit(solution)/shard_map/all_gather | solution.py:13
  20.4 1.3 %collective-permute-start.1 = (bf16[2,4,1,32,384]{4,3,2,1,0:T(8,128)(2,1)S(1)}, bf16[2,4,1,32,384]{4,3,2,1,0:T(8,128)(2,1)S(1)}, u32[]{:S(2)}, u32[]{:S(2)}) collective-permute-start(bf16[2,4,1,32,384]{4,3,2,1,0:T(8,128)(2,1)S(1)} %pad_maximum_fusion.9), channel_id=1, source_target_pairs={{1,0},{2,1},{3,2},{5,4},{6,5},{7,6},{9,8},{10,9},{11,10},{13,12},{... | collective-permute-start | bytes 589832 | tf_op jit(solution)/shard_map/ppermute | solution.py:42
  21.7 4.6 %collective-permute-start = (bf16[2,4,1,32,384]{4,3,2,1,0:T(8,128)(2,1)S(1)}, bf16[2,4,1,32,384]{4,3,2,1,0:T(8,128)(2,1)S(1)}, u32[]{:S(2)}, u32[]{:S(2)}) collective-permute-start(bf16[2,4,1,32,384]{4,3,2,1,0:T(8,128)(2,1)S(1)} %pad_maximum_fusion.9), channel_id=1, source_target_pairs={{0,1},{1,2},{2,3},{4,5},{5,6},{6,7},{8,9},{9,10},{10,11},{12,13},{... | collective-permute-start | bytes 589832 | tf_op jit(solution)/shard_map/ppermute | solution.py:40
  26.2 3.9 %fusion.29 = (bf16[1,1,3,384,384]{4,3,2,1,0:T(8,128)(2,1)S(1)}, bf16[1,1,3,384,384]{4,3,2,1,0:T(8,128)(2,1)S(1)}, bf16[1,1,3,384,384]{4,3,2,1,0:T(8,128)(2,1)S(1...) fusion(bf16[3,3,3,384,384]{4,3,2,1,0:T(8,128)(2,1)} %param.17), kind=kLoop, calls=%fused_computation.80 | loop fusion | bytes 15925248 | tf_op jit(solution)/shard_map/slice | solution.py:105
  30.2 0.6 collective-permute-done
  31.1 0.3 fusion.30
  32.3 0.3 convolution_add_fusion.8
  32.6 0.3 convolution_add_fusion.7
  33.3 0.3 convolution_add_fusion.5
  34.4 0.3 convolution_add_fusion.2
  34.8 0.5 copy-done.2
  35.5 11.4 %all_to_all.8 = bf16[4,1,1,32,384]{4,3,2,1,0:T(8,128)(2,1)S(1)} all-to-all(bf16[4,1,1,32,384]{4,3,2,1,0:T(8,128)(2,1)S(1)} %bitcast.111), channel_id=1, replica_groups=mesh['clips'=2,'tm'=4,'rows'=4] {'rows'}, dimensions={0} | all-to-all | bytes 196608 | tf_op jit(solution)/shard_map/all_to_all | solution.py:167
  46.9 0.3 fusion.1
  47.3 0.4 fusion.33
  47.7 1.0 %fusion.3 = bf16[128,384]{1,0:T(8,128)(2,1)} fusion(bf16[384,384]{1,0:T(8,128)(2,1)S(1)} %copy-done.1, f32[1,128,1152]{2,1,0:T(8,128)S(1)} %fusion.1, f32[384]{0:T(512)S(1)} %copy-done.6, f32[128,128]{0,1:T(8,128)S(1)} %get-tuple-element.117, f32[128]{0:T(128)S(1)} %fusion.24, f32[128]{0:T(128)S(1)} %get-tuple-element.116), kind=kOutput, calls=%fused_computation.20 | convolution fusion | flops 50528256 | bytes 560128 | tf_op jit(solution)/shard_map/dot_general | solution.py:132
  48.8 3.3 %all-to-all-start.1 = ((bf16[1,1,4,32,384]{4,3,1,0,2:T(8,128)(2,1)}), bf16[1,1,4,32,384]{4,3,1,0,2:T(8,128)(2,1)S(1)}, u32[]{:S(2)}, u32[]{:S(2)}) async-start(bf16[1,1,4,32,384]{4,3,1,0,2:T(8,128)(2,1)} %bitcast.35), calls=%async_computation.1 | async-start | bytes 196608 | tf_op jit(solution)/shard_map/all_to_all | solution.py:173
  52.2 5.7 %all-to-all-done.1 = bf16[1,1,4,32,384]{4,3,1,0,2:T(8,128)(2,1)S(1)} async-done(((bf16[1,1,4,32,384]{4,3,1,0,2:T(8,128)(2,1)}), bf16[1,1,4,32,384]{4,3,1,0,2:T(8,128)(2,1)S(1)}, u32[]{:S(2)}, u32[]{:S(2)}) %all-to-all-start.1) | async-done | bytes 98336 | tf_op jit(solution)/shard_map/all_to_all | solution.py:173
  57.9 0.7 %fusion.19 = bf16[2,2,1,32,384]{4,3,2,1,0:T(8,128)(2,1)} fusion(bf16[2,2,1,32,384]{4,3,2,1,0:T(8,128)(2,1)S(1)} %add_convert_fusion, bf16[2,2,1,32,384]{4,3,1,0,2:T(8,128)(2,1)S(1)} %bitcast.113, f32[2,2]{1,0:T(2,128)S(1)} %compare_convert_fusion), kind=kLoop, calls=%fused_computation.57 | loop fusion | flops 245760 | bytes 294928 | tf_op jit(solution)/shard_map/convert_element_type | solution.py:177
  (45 shorter events, 3.1 us)
Async XLA Ops:
  0.0 46.9 %copy-start = (bf16[384,1152]{1,0:T(8,128)(2,1)S(1)}, bf16[384,1152]{1,0:T(8,128)(2,1)}, u32[]{:S(2)}) copy-start(bf16[384,1152]{1,0:T(8,128)(2,1)} %param.20) | copy-start | bytes 2654212
  20.4 9.8 %collective-permute-start.1 = (bf16[2,4,1,32,384]{4,3,2,1,0:T(8,128)(2,1)S(1)}, bf16[2,4,1,32,384]{4,3,2,1,0:T(8,128)(2,1)S(1)}, u32[]{:S(2)}, u32[]{:S(2)}) collective-permute-start(bf16[2,4,1,32,384]{4,3,2,1,0:T(8,128)(2,1)S(1)} %pad_maximum_fusion.9), channel_id=1, source_target_pairs={{1,0},{2,1},{3,2},{5,4},{6,5},{7,6},{9,8},{10,9},{11,10},{13,12},{... | collective-permute-start | bytes 589832 | tf_op jit(solution)/shard_map/ppermute | solution.py:42
  21.7 9.1 %collective-permute-start = (bf16[2,4,1,32,384]{4,3,2,1,0:T(8,128)(2,1)S(1)}, bf16[2,4,1,32,384]{4,3,2,1,0:T(8,128)(2,1)S(1)}, u32[]{:S(2)}, u32[]{:S(2)}) collective-permute-start(bf16[2,4,1,32,384]{4,3,2,1,0:T(8,128)(2,1)S(1)} %pad_maximum_fusion.9), channel_id=1, source_target_pairs={{0,1},{1,2},{2,3},{4,5},{5,6},{6,7},{8,9},{9,10},{10,11},{12,13},{... | collective-permute-start | bytes 589832 | tf_op jit(solution)/shard_map/ppermute | solution.py:40
  34.4 0.9 %copy-start.2 = (bf16[2,2,1,32,384]{4,3,2,1,0:T(8,128)(2,1)S(1)}, bf16[2,2,1,32,384]{4,3,2,1,0:T(8,128)(2,1)}, u32[]{:S(2)}) copy-start(bf16[2,2,1,32,384]{4,3,2,1,0:T(8,128)(2,1)} %param.13) | copy-start | bytes 294916
  34.4 0.9 %copy-start.4 = (f32[384]{0:T(512)S(1)}, f32[384]{0:T(512)}, u32[]{:S(2)}) copy-start(f32[384]{0:T(512)} %param.18) | copy-start | bytes 4612
  34.4 1.0 %copy-start.5 = (f32[384]{0:T(512)S(1)}, f32[384]{0:T(512)}, u32[]{:S(2)}) copy-start(f32[384]{0:T(512)} %param.19) | copy-start | bytes 4612
  34.4 12.5 %copy-start.3 = (f32[1152]{0:T(1024)S(1)}, f32[1152]{0:T(1024)}, u32[]{:S(2)}) copy-start(f32[1152]{0:T(1024)} %param.21) | copy-start | bytes 13828
  35.2 12.5 %copy-start.1 = (bf16[384,384]{1,0:T(8,128)(2,1)S(1)}, bf16[384,384]{1,0:T(8,128)(2,1)}, u32[]{:S(2)}) copy-start(bf16[384,384]{1,0:T(8,128)(2,1)} %param.22) | copy-start | bytes 884740
  35.3 12.5 %copy-start.6 = (f32[384]{0:T(512)S(1)}, f32[384]{0:T(512)}, u32[]{:S(2)}) copy-start(f32[384]{0:T(512)} %param.23) | copy-start | bytes 4612
  46.9 5.2 %copy-start.7 = (s32[2,1]{0,1:T(1,128)S(1)}, s32[2,1]{0,1:T(1,128)}, u32[]{:S(2)}) copy-start(s32[2,1]{0,1:T(1,128)} %param.15) | copy-start | bytes 28
  48.8 9.1 %all-to-all-start.1 = ((bf16[1,1,4,32,384]{4,3,1,0,2:T(8,128)(2,1)}), bf16[1,1,4,32,384]{4,3,1,0,2:T(8,128)(2,1)S(1)}, u32[]{:S(2)}, u32[]{:S(2)}) async-start(bf16[1,1,4,32,384]{4,3,1,0,2:T(8,128)(2,1)} %bitcast.35), calls=%async_computation.1 | async-start | bytes 196608 | tf_op jit(solution)/shard_map/all_to_all | solution.py:173
where the time goes:
time: 59.1 us; the launch traced here: 58.6 us
  blocking collectives  25.9 us (44%)
  starting transfers between devices  9.15 us (15%)
  local copies, waits for them, and re-layouts  6.47 us (11%)
  waiting for transfers between devices  6.3 us (11%)
  other arithmetic  5.2 us (9%)
  matrix products  4.62 us (8%)
  between operations  0.98 us (2%)
    all_to_all x1, blocking collectives, body(): lax.all_to_all(grouped, 'rows', split_axis=0, concat_axis=2, tiled=True)  11.4 us
    unnamed x1, blocking collectives  8.31 us
    all_gather x1, blocking collectives, prefix(): gathered = jax.tree.map(lambda a: lax.all_gather(a, axis), part)  6.15 us
    all_to_all x1, waiting for transfers between devices, body(): lax.all_to_all(result, 'rows', split_axis=2, concat_axis=0, tiled=True)  5.72 us
    ppermute x1, starting transfers between devices, with_halo(): lax.ppermute(tail, axis, [(i, (i + 1) % count) for i in range(ends)])  4.56 us
    slice x1, local copies, waits for them, and re-layouts, convolve(): causal_weight[delta_time, delta_row].reshape(3 * channels, channels)  3.94 us
    all_to_all x1, starting transfers between devices, body(): lax.all_to_all(result, 'rows', split_axis=2, concat_axis=0, tiled=True)  3.3 us
    dot_general x9, matrix products, convolve(): jnp.dot(columns.reshape(-1, 3 * channels), kernel, preferred_element_type...  2.83 us
  transfers between devices with their start and end apart: 3, of which 2 were waited for; matrix products, arithmetic and copies ran while one was open for 7% of the time, Pallas kernels for 0%

commit v1 on v0

v1 whole, which is shorter than its diff:
```python
import functools
import math

import jax
import jax.numpy as jnp
from jax import lax
from jax.experimental import pallas as pl
from jax.experimental.pallas import tpu as pltpu
from jax.sharding import PartitionSpec as P

EPSILON = 1e-06


def loop(count, step):
    if count == 1:
        step(0)
    else:

        def one(index, carry):
            step(index)
            return carry

        lax.fori_loop(0, count, one, 0)


TAPS = ((2, 1), (2, 0), (2, 2), (1, 1), (0, 1), (1, 0), (1, 2), (0, 0), (0, 2))
STAGES = ((0, 3), (3, 5), (5, 9))


def segment_kernel(
    n_tm,
    n_rows,
    clips,
    cols,
    ch,
    seg_ref,
    inner_ref,
    len_ref,
    inner_gain_ref,
    weight_ref,
    conv_bias_ref,
    attn_gain_ref,
    triple_ref,
    triple_bias_ref,
    output_ref,
    output_bias_ref,
    out_ref,
    ext,
    prev,
    prev2,
    last,
    flag_out,
    flag_in,
    wbuf,
    tbuf,
    obuf,
    conv,
    residual,
    normed,
    gathered,
    kbuf,
    vbuf,
    result,
    returned,
    wsem,
    psem,
    near_send,
    near_recv,
    tm_send,
    tm_recv,
    to_send,
    to_recv,
    back_send,
    back_recv,
):
    s = lax.axis_index("tm")
    r = lax.axis_index("rows")
    frames = 2 * clips
    per = frames // n_rows
    chunk = min(frames, 4)
    bf16, f32 = jnp.bfloat16, jnp.float32

    for i, (kt, kh) in enumerate(TAPS):
        for kw in range(3):
            pltpu.make_async_copy(
                weight_ref.at[kt, kh, kw],
                wbuf.at[pl.ds(i * ch, ch), pl.ds(kw * ch, ch)],
                wsem.at[i],
            ).start()
    triple_copy = pltpu.make_async_copy(triple_ref, tbuf, psem.at[0])
    output_copy = pltpu.make_async_copy(output_ref, obuf, psem.at[1])
    triple_copy.start()
    output_copy.start()

    barrier = pltpu.get_barrier_semaphore()
    for k in range(1, n_rows):
        pl.semaphore_signal(
            barrier,
            inc=1,
            device_id={"rows": lax.rem(r + k, n_rows)},
            device_id_type=pl.DeviceIdType.MESH,
        )
    expected = n_rows - 1
    for k in (-2, -1, 1, 2):
        there = jnp.logical_and(s + k >= 0, s + k < n_tm)
        expected = expected + there.astype(jnp.int32)

        @pl.when(there)
        def _():
            pl.semaphore_signal(
                barrier, inc=1, device_id={"tm": s + k}, device_id_type=pl.DeviceIdType.MESH
            )

    for b in range(clips):
        for t in range(2):
            field = inner_ref[b, t, 0].astype(f32)
            mean = jnp.mean(field * field, axis=-1, keepdims=True)
            v = field * lax.rsqrt(mean + EPSILON) * inner_gain_ref[...]
            ext[1, (2 + t) * clips + b] = (v / (1.0 + jnp.exp(-v))).astype(bf16)
        count = len_ref[b, 0]
        both = count == 2
        first = ext[1, 2 * clips + b].astype(f32)
        second = ext[1, 3 * clips + b].astype(f32)
        last[b] = jnp.where(both, second, first).astype(bf16)
        flag_out[b] = jnp.full((8, ch), count.astype(f32), f32)

    own = pl.ds(2 * clips, 2 * clips)
    cached = pl.ds(0, 2 * clips)
    blank = jnp.zeros((2 * clips, cols, ch), bf16)

    @pl.when(r == 0)
    def _():
        ext[0] = jnp.zeros((4 * clips, cols, ch), bf16)

    @pl.when(r == n_rows - 1)
    def _():
        ext[2] = jnp.zeros((4 * clips, cols, ch), bf16)

    @pl.when(s == 0)
    def _():
        ext[1, cached] = blank
        prev[...] = blank
        flag_in[...] = jnp.zeros((clips, 8, ch), f32)

        @pl.when(r > 0)
        def _():
            ext[0, cached] = blank

        @pl.when(r < n_rows - 1)
        def _():
            ext[2, cached] = blank

    @pl.when(s <= 1)
    def _():
        prev2[...] = jnp.zeros((clips, cols, ch), bf16)

    def remote(src, dst, send, recv, where):
        return pltpu.make_async_remote_copy(
            src_ref=src,
            dst_ref=dst,
            send_sem=send,
            recv_sem=recv,
            device_id=where,
            device_id_type=pl.DeviceIdType.MESH,
        )

    down, up = {"rows": r + 1}, {"rows": r - 1}
    has_down, has_up = r < n_rows - 1, r > 0
    own_down = remote(ext.at[1, own], ext.at[0, own], near_send.at[0], near_recv.at[0], down)
    own_up = remote(ext.at[1, own], ext.at[2, own], near_send.at[1], near_recv.at[1], up)
    old_down = remote(ext.at[1, cached], ext.at[0, cached], near_send.at[2], near_recv.at[2], down)
    old_up = remote(ext.at[1, cached], ext.at[2, cached], near_send.at[3], near_recv.at[3], up)
    to_next = remote(ext.at[1, own], prev, tm_send.at[0], tm_recv.at[0], {"tm": s + 1})
    to_flag = remote(flag_out, flag_in, tm_send.at[1], tm_recv.at[1], {"tm": s + 1})
    to_after = remote(last, prev2, tm_send.at[2], tm_recv.at[2], {"tm": s + 2})

    pl.semaphore_wait(barrier, expected)

    @pl.when(s + 1 < n_tm)
    def _():
        to_flag.start()
        to_next.start()

    @pl.when(s + 2 < n_tm)
    def _():
        to_after.start()

    @pl.when(has_down)
    def _():
        own_down.start()

    @pl.when(has_up)
    def _():
        own_up.start()

    @pl.when(s > 0)
    def _():
        to_flag.wait_recv()
        to_next.wait_recv()

        @pl.when(s > 1)
        def _():
            to_after.wait_recv()

        for b in range(clips):
            both = flag_in[b, 0:1, :] > 1.5
            first = prev[b].astype(f32)
            second = prev[clips + b].astype(f32)
            older = prev2[b].astype(f32)
            ext[1, clips + b] = jnp.where(both, second, first).astype(bf16)
            ext[1, b] = jnp.where(both, first, older).astype(bf16)

        @pl.when(has_down)
        def _():
            old_down.start()

        @pl.when(has_up)
        def _():
            old_up.start()

    def taps_dot(stage, at):
        begin, end = STAGES[stage]
        parts = [
            ext[kh, pl.ds(kt * clips + at * chunk, chunk)].reshape(chunk * cols, ch)
            for kt, kh in TAPS[begin:end]
        ]
        return jnp.dot(
            jnp.concatenate(parts, axis=-1),
            wbuf[begin * ch : end * ch, :],
            preferred_element_type=f32,
        )

    def weights_here(stage):
        for i in range(*STAGES[stage]):
            rows = wbuf.at[pl.ds(i * ch, ch)]
            pltpu.make_async_copy(rows, rows, wsem.at[i]).wait()

    @pl.when(has_up)
    def _():
        own_down.wait_recv()

    @pl.when(has_down)
    def _():
        own_up.wait_recv()

    weights_here(0)
    weights_here(1)

    def early(at):
        conv[at] = taps_dot(0, at) + taps_dot(1, at)

    loop(frames // chunk, early)
    weights_here(2)

    @pl.when(s > 0)
    def _():
        @pl.when(has_up)
        def _():
            old_down.wait_recv()

        @pl.when(has_down)
        def _():
            old_up.wait_recv()

    def late(at):
        total = conv[at] + taps_dot(2, at)
        places = chunk * cols
        column = lax.rem(lax.broadcasted_iota(jnp.int32, (places, ch), 0), cols)
        left = pltpu.roll(total[:, :ch], 1, 0)
        right = pltpu.roll(total[:, 2 * ch :], places - 1, 0)
        summed = total[:, ch : 2 * ch] + jnp.where(column == 0, 0.0, left)
        summed = summed + jnp.where(column == cols - 1, 0.0, right)
        summed = summed + conv_bias_ref[...]
        at_frames = pl.ds(at * chunk, chunk)
        held = residual[at_frames].reshape(places, ch).astype(f32)
        held = (held + summed).astype(bf16)
        residual[at_frames] = held.reshape(chunk, cols, ch)
        wide = held.astype(f32)
        mean = jnp.mean(wide * wide, axis=-1, keepdims=True)
        wide = (wide * lax.rsqrt(mean + EPSILON) * attn_gain_ref[...]).astype(bf16)
        normed[at_frames] = wide.reshape(chunk, cols, ch)

    for b in range(clips):
        for t in range(2):
            residual[t * clips + b] = seg_ref[b, t, 0]
    loop(frames // chunk, late)

    there = []
    for k in range(1, n_rows):
        peer = lax.rem(r + k, n_rows)
        copy = remote(
            normed.at[pl.ds(peer * per, per)],
            gathered.at[r],
            to_send.at[k - 1],
            to_recv.at[k - 1],
            {"rows": peer},
        )
        copy.start()
        there.append(copy)
    gathered[r] = normed[pl.ds(r * per, per)]
    triple_copy.wait()
    output_copy.wait()
    for copy in there:
        copy.wait_recv()

    groups = max(1, n_rows * cols // 128)
    height = n_rows // groups

    for frame in range(per):

        def project(at):
            x = gathered[pl.ds(at * height, height), frame].reshape(height * cols, ch)
            packed = jnp.dot(x, tbuf[:, ch:], preferred_element_type=f32)
            packed = packed + triple_bias_ref[:, ch:]
            rows = pl.ds(at * height * cols, height * cols)
            kbuf[rows] = packed[:, :ch]
            vbuf[rows] = packed[:, ch:].astype(bf16)

        def attend_rows(at):
            x = gathered[pl.ds(at * height, height), frame].reshape(height * cols, ch)
            queries = jnp.dot(x, tbuf[:, :ch], preferred_element_type=f32)
            queries = queries + triple_bias_ref[:, :ch]
            scores = lax.dot_general(
                queries,
                kbuf[...],
                (((1,), (1,)), ((), ())),
                precision=lax.Precision.HIGHEST,
                preferred_element_type=f32,
            ) / math.sqrt(ch)
            exponent = jnp.exp(scores - jnp.max(scores, axis=-1, keepdims=True))
            weights = (exponent / jnp.sum(exponent, axis=-1, keepdims=True)).astype(bf16)
            attended = jnp.dot(weights, vbuf[...], preferred_element_type=f32).astype(bf16)
            projected = jnp.dot(attended, obuf[...], preferred_element_type=f32)
            projected = (projected + output_bias_ref[...]).astype(bf16)
            result[pl.ds(at * height, height), frame] = projected.reshape(height, cols, ch)

        loop(groups, project)
        loop(groups, attend_rows)

    back = []
    for k in range(1, n_rows):
        peer = lax.rem(r + k, n_rows)
        copy = remote(
            result.at[peer],
            returned.at[pl.ds(r * per, per)],
            back_send.at[k - 1],
            back_recv.at[k - 1],
            {"rows": peer},
        )
        copy.start()
        back.append(copy)
    returned[pl.ds(r * per, per)] = result[r]
    for copy in back:
        copy.wait_recv()

    for b in range(clips):
        count = len_ref[b, 0]
        for t in range(2):
            f = t * clips + b
            live = (count > t).astype(f32)
            summed = residual[f].astype(f32) + returned[f].astype(f32)
            out_ref[b, t, 0] = (summed * live).astype(bf16)

    for copy in there + back:
        copy.wait_send()

    @pl.when(s + 1 < n_tm)
    def _():
        to_flag.wait_send()
        to_next.wait_send()

    @pl.when(s + 2 < n_tm)
    def _():
        to_after.wait_send()

    @pl.when(has_down)
    def _():
        own_down.wait_send()

    @pl.when(has_up)
    def _():
        own_up.wait_send()

    @pl.when(s > 0)
    def _():
        @pl.when(has_down)
        def _():
            old_down.wait_send()

        @pl.when(has_up)
        def _():
            old_up.wait_send()


def segment(
    n_tm,
    n_rows,
    segment_input,
    inner_input,
    lengths,
    inner_gain,
    causal_weight,
    causal_bias,
    attention_gain,
    triple_weight,
    triple_bias,
    output_weight,
    output_bias,
):
    clips, _, _, cols, ch = segment_input.shape
    frames = 2 * clips
    per = frames // n_rows
    chunk = min(frames, 4)
    bf16, f32 = jnp.bfloat16, jnp.float32
    vmem = pl.BlockSpec(memory_space=pltpu.VMEM)
    hbm = pl.BlockSpec(memory_space=pl.ANY)
    smem = pl.BlockSpec(memory_space=pltpu.SMEM)
    dma = pltpu.SemaphoreType.DMA
    return pl.pallas_call(
        functools.partial(segment_kernel, n_tm, n_rows, clips, cols, ch),
        out_shape=jax.ShapeDtypeStruct(segment_input.shape, bf16),
        in_specs=[vmem, vmem, smem, vmem, hbm, vmem, vmem, hbm, vmem, hbm, vmem],
        out_specs=vmem,
        scratch_shapes=[
            pltpu.VMEM((3, 4 * clips, cols, ch), bf16),
            pltpu.VMEM((2 * clips, cols, ch), bf16),
            pltpu.VMEM((clips, cols, ch), bf16),
            pltpu.VMEM((clips, cols, ch), bf16),
            pltpu.VMEM((clips, 8, ch), f32),
            pltpu.VMEM((clips, 8, ch), f32),
            pltpu.VMEM((9 * ch, 3 * ch), bf16),
            pltpu.VMEM((ch, 3 * ch), bf16),
            pltpu.VMEM((ch, ch), bf16),
            pltpu.VMEM((frames // chunk, chunk * cols, 3 * ch), f32),
            pltpu.VMEM((frames, cols, ch), bf16),
            pltpu.VMEM((frames, cols, ch), bf16),
            pltpu.VMEM((n_rows, per, cols, ch), bf16),
            pltpu.VMEM((n_rows * cols, ch), f32),
            pltpu.VMEM((n_rows * cols, ch), bf16),
            pltpu.VMEM((n_rows, per, cols, ch), bf16),
            pltpu.VMEM((frames, cols, ch), bf16),
            dma((9,)),
            dma((2,)),
            dma((4,)),
            dma((4,)),
            dma((3,)),
            dma((3,)),
            dma((n_rows - 1,)),
            dma((n_rows - 1,)),
            dma((n_rows - 1,)),
            dma((n_rows - 1,)),
        ],
        compiler_params=pltpu.CompilerParams(
            collective_id=0, has_side_effects=True, vmem_limit_bytes=56 * 1024 * 1024
        ),
        name="segment",
    )(
        segment_input,
        inner_input,
        lengths,
        inner_gain[None],
        causal_weight,
        causal_bias[None],
        attention_gain[None],
        triple_weight,
        triple_bias[None],
        output_weight,
        output_bias[None],
    )


def solution(mesh):
    placed = (
        P("clips", "tm", "rows", None, None),
        P("clips", "tm", "rows", None, None),
        P("clips", "tm"),
        P(),
        P(),
        P(),
        P(),
        P(),
        P(),
        P(),
        P(),
    )
    return jax.shard_map(
        functools.partial(segment, mesh.shape["tm"], mesh.shape["rows"]),
        mesh=mesh,
        in_specs=placed,
        out_specs=P("clips", "tm", "rows", None, None),
        check_vma=False,
    )
```

time: 59.1 us -> 32.3 us (0.55)
  the two profiles are of different devices: /device:TPU:0 before, /device:TPU:2 now
where the time goes in v1:
time: 32.3 us; the launch traced here: 32 us
  Pallas kernels  22.8 us (71%)
  local copies, waits for them, and re-layouts  9.21 us (29%)
    pallas_call x1, Pallas kernels, segment(): pl.pallas_call(functools.partial(segment_kernel, n_tm, n_rows, clips, col...  22.8 us
    unnamed x2, local copies, waits for them, and re-layouts  2.84 us
    broadcast_in_dim x1, local copies, waits for them, and re-layouts, segment(): triple_bias[None]  1.29 us
    broadcast_in_dim x1, local copies, waits for them, and re-layouts, segment(): inner_gain[None]  1.28 us
    broadcast_in_dim x1, local copies, waits for them, and re-layouts, segment(): causal_bias[None]  1.27 us
    broadcast_in_dim x1, local copies, waits for them, and re-layouts, segment(): attention_gain[None]  1.27 us
    broadcast_in_dim x1, local copies, waits for them, and re-layouts, segment(): output_bias[None]  1.26 us

profile of v1, /device:TPU:2, one launch (start us, length us, event | category | flops | bytes accessed | tf_op | source)
XLA Modules:
  0.0 32.0 jit_solution(6035489613163888842)
XLA Ops:
  0.0 1.3 %copy.12.len_ref = s32[2,1]{1,0:T(2,128)} copy(s32[2,1]{0,1:T(1,128)} %param.13) | data formatting | bytes 16 | tf_op args[2]
  1.3 1.3 %broadcast_in_dim.15.inner_gain_ref = f32[1,384]{1,0:T(1,128)} reshape(f32[384]{0:T(512)} %param.14) | data formatting | bytes 3072 | tf_op jit(solution)/shard_map/broadcast_in_dim | solution.py:461
  2.6 1.3 %broadcast_in_dim.16.conv_bias_ref = f32[1,384]{1,0:T(1,128)} reshape(f32[384]{0:T(512)} %param.16) | data formatting | bytes 3072 | tf_op jit(solution)/shard_map/broadcast_in_dim | solution.py:463
  3.8 1.3 %broadcast_in_dim.17.attn_gain_ref = f32[1,384]{1,0:T(1,128)} reshape(f32[384]{0:T(512)} %param.17) | data formatting | bytes 3072 | tf_op jit(solution)/shard_map/broadcast_in_dim | solution.py:464
  5.1 1.3 %broadcast_in_dim.19.output_bias_ref = f32[1,384]{1,0:T(1,128)} reshape(f32[384]{0:T(512)} %param.21) | data formatting | bytes 3072 | tf_op jit(solution)/shard_map/broadcast_in_dim | solution.py:468
  6.4 1.3 %broadcast_in_dim.18.triple_bias_ref = f32[1,1152]{1,0:T(1,128)} reshape(f32[1152]{0:T(1024)} %param.19) | data formatting | bytes 9216 | tf_op jit(solution)/shard_map/broadcast_in_dim | solution.py:466
  7.7 22.8 %segment.1 = bf16[2,2,1,32,384]{4,3,2,1,0:T(8,128)(2,1)} custom-call(bf16[2,2,1,32,384]{4,3,2,1,0:T(8,128)(2,1)} %seg_ref.1, bf16[2,2,1,32,384]{4,3,2,1,0:T(8,128)(2,1)} %inner_ref.1, s32[2,1]{1,0:T(2,128)} %copy.12.len_ref, f32[1,384]{1,0:T(1,128)} %broadcast_in_dim.15.inner_gain_ref, bf16[3,3,3,384,384]{4,3,2,1,0:T(8,128)(2,1)} %weight_ref.1, ...), custom_call_target="tpu_custom_call" | custom-call | tf_op jit(solution)/shard_map/segment/pallas_call | solution.py:419
  30.4 1.5 %copy.14 = bf16[2,2,1,32,384]{4,3,2,1,0:T(8,128)(2,1)} copy(bf16[2,2,1,32,384]{4,3,2,1,0:T(8,128)(2,1)} %segment.1) | data formatting | bytes 196608

commit v2 on v1

--- a/solution.py
+++ b/solution.py
@@ -33,18 +33,27 @@
     clips,
     cols,
     ch,
+    seg_any,
+    inner_any,
+    len_any,
+    inner_gain_any,
+    weight_ref,
+    conv_bias_any,
+    attn_gain_any,
+    triple_ref,
+    triple_bias_any,
+    output_ref,
+    output_bias_any,
+    out_ref,
     seg_ref,
     inner_ref,
     len_ref,
     inner_gain_ref,
-    weight_ref,
     conv_bias_ref,
     attn_gain_ref,
-    triple_ref,
     triple_bias_ref,
-    output_ref,
     output_bias_ref,
-    out_ref,
+    insem,
     ext,
     prev,
     prev2,
@@ -80,18 +89,6 @@
     chunk = min(frames, 4)
     bf16, f32 = jnp.bfloat16, jnp.float32
 
-    for i, (kt, kh) in enumerate(TAPS):
-        for kw in range(3):
-            pltpu.make_async_copy(
-                weight_ref.at[kt, kh, kw],
-                wbuf.at[pl.ds(i * ch, ch), pl.ds(kw * ch, ch)],
-                wsem.at[i],
-            ).start()
-    triple_copy = pltpu.make_async_copy(triple_ref, tbuf, psem.at[0])
-    output_copy = pltpu.make_async_copy(output_ref, obuf, psem.at[1])
-    triple_copy.start()
-    output_copy.start()
-
     barrier = pltpu.get_barrier_semaphore()
     for k in range(1, n_rows):
         pl.semaphore_signal(
@@ -111,13 +108,47 @@
                 barrier, inc=1, device_id={"tm": s + k}, device_id_type=pl.DeviceIdType.MESH
             )
 
+    small = [
+        pltpu.make_async_copy(src, dst, insem.at[i])
+        for i, (src, dst) in enumerate(
+            (
+                (inner_any, inner_ref),
+                (inner_gain_any, inner_gain_ref),
+                (len_any, len_ref),
+                (seg_any, seg_ref),
+                (conv_bias_any, conv_bias_ref),
+                (attn_gain_any, attn_gain_ref),
+                (triple_bias_any, triple_bias_ref),
+                (output_bias_any, output_bias_ref),
+            )
+        )
+    ]
+    for copy in small:
+        copy.start()
+
+    for i, (kt, kh) in enumerate(TAPS):
+        for kw in range(3):
+            pltpu.make_async_copy(
+                weight_ref.at[kt, kh, kw],
+                wbuf.at[pl.ds(i * ch, ch), pl.ds(kw * ch, ch)],
+                wsem.at[i],
+            ).start()
+    triple_copy = pltpu.make_async_copy(triple_ref, tbuf, psem.at[0])
+    output_copy = pltpu.make_async_copy(output_ref, obuf, psem.at[1])
+    triple_copy.start()
+    output_copy.start()
+
+    for copy in small[:3]:
+        copy.wait()
+    inner_gain = inner_gain_ref[...].reshape(1, ch)
+
     for b in range(clips):
         for t in range(2):
             field = inner_ref[b, t, 0].astype(f32)
             mean = jnp.mean(field * field, axis=-1, keepdims=True)
-            v = field * lax.rsqrt(mean + EPSILON) * inner_gain_ref[...]
+            v = field * lax.rsqrt(mean + EPSILON) * inner_gain
             ext[1, (2 + t) * clips + b] = (v / (1.0 + jnp.exp(-v))).astype(bf16)
-        count = len_ref[b, 0]
+        count = len_ref[0, b]
         both = count == 2
         first = ext[1, 2 * clips + b].astype(f32)
         second = ext[1, 3 * clips + b].astype(f32)
@@ -262,6 +293,13 @@
         def _():
             old_up.wait_recv()
 
+    for copy in small[3:]:
+        copy.wait()
+    conv_bias = conv_bias_ref[...].reshape(1, ch)
+    attn_gain = attn_gain_ref[...].reshape(1, ch)
+    triple_bias = triple_bias_ref[...].reshape(1, 3 * ch)
+    output_bias = output_bias_ref[...].reshape(1, ch)
+
     def late(at):
         total = conv[at] + taps_dot(2, at)
         places = chunk * cols
@@ -270,14 +308,14 @@
         right = pltpu.roll(total[:, 2 * ch :], places - 1, 0)
         summed = total[:, ch : 2 * ch] + jnp.where(column == 0, 0.0, left)
         summed = summed + jnp.where(column == cols - 1, 0.0, right)
-        summed = summed + conv_bias_ref[...]
+        summed = summed + conv_bias
         at_frames = pl.ds(at * chunk, chunk)
         held = residual[at_frames].reshape(places, ch).astype(f32)
         held = (held + summed).astype(bf16)
         residual[at_frames] = held.reshape(chunk, cols, ch)
         wide = held.astype(f32)
         mean = jnp.mean(wide * wide, axis=-1, keepdims=True)
-        wide = (wide * lax.rsqrt(mean + EPSILON) * attn_gain_ref[...]).astype(bf16)
+        wide = (wide * lax.rsqrt(mean + EPSILON) * attn_gain).astype(bf16)
         normed[at_frames] = wide.reshape(chunk, cols, ch)
 
     for b in range(clips):
@@ -311,7 +349,7 @@
         def project(at):
             x = gathered[pl.ds(at * height, height), frame].reshape(height * cols, ch)
             packed = jnp.dot(x, tbuf[:, ch:], preferred_element_type=f32)
-            packed = packed + triple_bias_ref[:, ch:]
+            packed = packed + triple_bias[:, ch:]
             rows = pl.ds(at * height * cols, height * cols)
             kbuf[rows] = packed[:, :ch]
             vbuf[rows] = packed[:, ch:].astype(bf16)
@@ -319,7 +357,7 @@
         def attend_rows(at):
             x = gathered[pl.ds(at * height, height), frame].reshape(height * cols, ch)
             queries = jnp.dot(x, tbuf[:, :ch], preferred_element_type=f32)
-            queries = queries + triple_bias_ref[:, :ch]
+            queries = queries + triple_bias[:, :ch]
             scores = lax.dot_general(
                 queries,
                 kbuf[...],
@@ -331,7 +369,7 @@
             weights = (exponent / jnp.sum(exponent, axis=-1, keepdims=True)).astype(bf16)
             attended = jnp.dot(weights, vbuf[...], preferred_element_type=f32).astype(bf16)
             projected = jnp.dot(attended, obuf[...], preferred_element_type=f32)
-            projected = (projected + output_bias_ref[...]).astype(bf16)
+            projected = (projected + output_bias).astype(bf16)
             result[pl.ds(at * height, height), frame] = projected.reshape(height, cols, ch)
 
         loop(groups, project)
@@ -354,7 +392,7 @@
         copy.wait_recv()
 
     for b in range(clips):
-        count = len_ref[b, 0]
+        count = len_ref[0, b]
         for t in range(2):
             f = t * clips + b
             live = (count > t).astype(f32)
@@ -414,14 +452,22 @@
     bf16, f32 = jnp.bfloat16, jnp.float32
     vmem = pl.BlockSpec(memory_space=pltpu.VMEM)
     hbm = pl.BlockSpec(memory_space=pl.ANY)
-    smem = pl.BlockSpec(memory_space=pltpu.SMEM)
     dma = pltpu.SemaphoreType.DMA
     return pl.pallas_call(
         functools.partial(segment_kernel, n_tm, n_rows, clips, cols, ch),
         out_shape=jax.ShapeDtypeStruct(segment_input.shape, bf16),
-        in_specs=[vmem, vmem, smem, vmem, hbm, vmem, vmem, hbm, vmem, hbm, vmem],
+        in_specs=[hbm] * 11,
         out_specs=vmem,
         scratch_shapes=[
+            pltpu.VMEM(segment_input.shape, bf16),
+            pltpu.VMEM(inner_input.shape, bf16),
+            pltpu.SMEM((1, clips), jnp.int32),
+            pltpu.VMEM((ch,), f32),
+            pltpu.VMEM((ch,), f32),
+            pltpu.VMEM((ch,), f32),
+            pltpu.VMEM((3 * ch,), f32),
+            pltpu.VMEM((ch,), f32),
+            dma((8,)),
             pltpu.VMEM((3, 4 * clips, cols, ch), bf16),
             pltpu.VMEM((2 * clips, cols, ch), bf16),
             pltpu.VMEM((clips, cols, ch), bf16),
@@ -457,15 +503,15 @@
     )(
         segment_input,
         inner_input,
-        lengths,
-        inner_gain[None],
+        lengths.T,
+        inner_gain,
         causal_weight,
-        causal_bias[None],
-        attention_gain[None],
+        causal_bias,
+        attention_gain,
         triple_weight,
-        triple_bias[None],
+        triple_bias,
         output_weight,
-        output_bias[None],
+        output_bias,
     )
 
 

time: 32.3 us -> 24.4 us (0.76)
  local copies, waits for them, and re-layouts: 9.21 us -> 1.54 us
    broadcast_in_dim x5 -> x0, local copies, waits for them, and re-layouts: 6.37 us -> none  [the longest x1 1.29 us: segment(): triple_bias[None]]
    unnamed x2 -> x1, local copies, waits for them, and re-layouts: 2.84 us -> 1.54 us
where the time goes in v2:
time: 24.4 us; the launch traced here: 24.2 us
  Pallas kernels  22.7 us (93%)
  local copies, waits for them, and re-layouts  1.54 us (6%)
    pallas_call x1, Pallas kernels, segment(): pl.pallas_call(functools.partial(segment_kernel, n_tm, n_rows, clips, col...  22.7 us
    unnamed x1, local copies, waits for them, and re-layouts  1.54 us

profile of v2, /device:TPU:2, one launch (start us, length us, event | category | flops | bytes accessed | tf_op | source)
XLA Modules:
  0.0 24.2 jit_solution(1220318244253461227)
XLA Ops:
  0.0 22.7 %segment.1 = bf16[2,2,1,32,384]{4,3,2,1,0:T(8,128)(2,1)} custom-call(bf16[2,2,1,32,384]{4,3,2,1,0:T(8,128)(2,1)} %seg_any.1, bf16[2,2,1,32,384]{4,3,2,1,0:T(8,128)(2,1)} %inner_any.1, s32[1,2]{1,0:T(1,128)} %bitcast.1, f32[384]{0:T(512)} %inner_gain_any.1, bf16[3,3,3,384,384]{4,3,2,1,0:T(8,128)(2,1)} %weight_ref.1, f32[384]{0:T(512)} %conv_bias_any.1, ...), custom_call_target="tpu_custom_call" | custom-call | tf_op jit(solution)/shard_map/segment/pallas_call | solution.py:456
  22.7 1.5 %copy.13 = bf16[2,2,1,32,384]{4,3,2,1,0:T(8,128)(2,1)} copy(bf16[2,2,1,32,384]{4,3,2,1,0:T(8,128)(2,1)} %segment.1) | data formatting | bytes 196608

commit v3 on v2

--- a/solution.py
+++ b/solution.py
@@ -23,8 +23,8 @@
         lax.fori_loop(0, count, one, 0)
 
 
-TAPS = ((2, 1), (2, 0), (2, 2), (1, 1), (0, 1), (1, 0), (1, 2), (0, 0), (0, 2))
-STAGES = ((0, 3), (3, 5), (5, 9))
+TAPS = ((2, 1), (1, 1), (0, 1), (2, 0), (2, 2), (1, 0), (1, 2), (0, 0), (0, 2))
+STAGES = ((0, 1), (1, 3), (3, 5), (5, 9))
 
 
 def segment_kernel(
@@ -86,7 +86,10 @@
     r = lax.axis_index("rows")
     frames = 2 * clips
     per = frames // n_rows
-    chunk = min(frames, 4)
+    chunk = 2 - clips % 2
+    places = 2 * chunk * cols
+    halves = 2 if clips % 2 == 0 else 1
+    share = clips // halves
     bf16, f32 = jnp.bfloat16, jnp.float32
 
     barrier = pltpu.get_barrier_semaphore()
@@ -147,39 +150,38 @@
             field = inner_ref[b, t, 0].astype(f32)
             mean = jnp.mean(field * field, axis=-1, keepdims=True)
             v = field * lax.rsqrt(mean + EPSILON) * inner_gain
-            ext[1, (2 + t) * clips + b] = (v / (1.0 + jnp.exp(-v))).astype(bf16)
+            ext[1, b, 2 + t] = (v / (1.0 + jnp.exp(-v))).astype(bf16)
         count = len_ref[0, b]
         both = count == 2
-        first = ext[1, 2 * clips + b].astype(f32)
-        second = ext[1, 3 * clips + b].astype(f32)
+        first = ext[1, b, 2].astype(f32)
+        second = ext[1, b, 3].astype(f32)
         last[b] = jnp.where(both, second, first).astype(bf16)
         flag_out[b] = jnp.full((8, ch), count.astype(f32), f32)
 
-    own = pl.ds(2 * clips, 2 * clips)
-    cached = pl.ds(0, 2 * clips)
-    blank = jnp.zeros((2 * clips, cols, ch), bf16)
+    own, cached = pl.ds(2, 2), pl.ds(0, 2)
+    blank = jnp.zeros((clips, 2, cols, ch), bf16)
 
     @pl.when(r == 0)
     def _():
-        ext[0] = jnp.zeros((4 * clips, cols, ch), bf16)
+        ext[0] = jnp.zeros((clips, 4, cols, ch), bf16)
 
     @pl.when(r == n_rows - 1)
     def _():
-        ext[2] = jnp.zeros((4 * clips, cols, ch), bf16)
+        ext[2] = jnp.zeros((clips, 4, cols, ch), bf16)
 
     @pl.when(s == 0)
     def _():
-        ext[1, cached] = blank
+        ext[1, :, cached] = blank
         prev[...] = blank
         flag_in[...] = jnp.zeros((clips, 8, ch), f32)
 
         @pl.when(r > 0)
         def _():
-            ext[0, cached] = blank
+            ext[0, :, cached] = blank
 
         @pl.when(r < n_rows - 1)
         def _():
-            ext[2, cached] = blank
+            ext[2, :, cached] = blank
 
     @pl.when(s <= 1)
     def _():
@@ -197,24 +199,43 @@
 
     down, up = {"rows": r + 1}, {"rows": r - 1}
     has_down, has_up = r < n_rows - 1, r > 0
-    own_down = remote(ext.at[1, own], ext.at[0, own], near_send.at[0], near_recv.at[0], down)
-    own_up = remote(ext.at[1, own], ext.at[2, own], near_send.at[1], near_recv.at[1], up)
-    old_down = remote(ext.at[1, cached], ext.at[0, cached], near_send.at[2], near_recv.at[2], down)
-    old_up = remote(ext.at[1, cached], ext.at[2, cached], near_send.at[3], near_recv.at[3], up)
-    to_next = remote(ext.at[1, own], prev, tm_send.at[0], tm_recv.at[0], {"tm": s + 1})
-    to_flag = remote(flag_out, flag_in, tm_send.at[1], tm_recv.at[1], {"tm": s + 1})
-    to_after = remote(last, prev2, tm_send.at[2], tm_recv.at[2], {"tm": s + 2})
+    own_down = remote(ext.at[1, :, own], ext.at[0, :, own], near_send.at[0], near_recv.at[0], down)
+    own_up = remote(ext.at[1, :, own], ext.at[2, :, own], near_send.at[1], near_recv.at[1], up)
+    to_flag = remote(flag_out, flag_in, tm_send.at[0], tm_recv.at[0], {"tm": s + 1})
+    old_down, old_up, to_next, to_after = [], [], [], []
+    for g in range(halves):
+        part = pl.ds(g * share, share)
+        mine = ext.at[1, part, cached]
+        i, j = 2 + 2 * g, 3 + 2 * g
+        old_down.append(
+            remote(mine, ext.at[0, part, cached], near_send.at[i], near_recv.at[i], down)
+        )
+        old_up.append(remote(mine, ext.at[2, part, cached], near_send.at[j], near_recv.at[j], up))
+        i, j = 1 + 2 * g, 2 + 2 * g
+        to_next.append(
+            remote(
+                ext.at[1, part, own], prev.at[part], tm_send.at[i], tm_recv.at[i], {"tm": s + 1}
+            )
+        )
+        to_after.append(
+            remote(last.at[part], prev2.at[part], tm_send.at[j], tm_recv.at[j], {"tm": s + 2})
+        )
 
     pl.semaphore_wait(barrier, expected)
 
     @pl.when(s + 1 < n_tm)
     def _():
         to_flag.start()
-        to_next.start()
-
-    @pl.when(s + 2 < n_tm)
-    def _():
-        to_after.start()
+
+    for g in range(halves):
+
+        @pl.when(s + 1 < n_tm)
+        def _():
+            to_next[g].start()
+
+        @pl.when(s + 2 < n_tm)
+        def _():
+            to_after[g].start()
 
     @pl.when(has_down)
     def _():
@@ -223,36 +244,11 @@
     @pl.when(has_up)
     def _():
         own_up.start()
-
-    @pl.when(s > 0)
-    def _():
-        to_flag.wait_recv()
-        to_next.wait_recv()
-
-        @pl.when(s > 1)
-        def _():
-            to_after.wait_recv()
-
-        for b in range(clips):
-            both = flag_in[b, 0:1, :] > 1.5
-            first = prev[b].astype(f32)
-            second = prev[clips + b].astype(f32)
-            older = prev2[b].astype(f32)
-            ext[1, clips + b] = jnp.where(both, second, first).astype(bf16)
-            ext[1, b] = jnp.where(both, first, older).astype(bf16)
-
-        @pl.when(has_down)
-        def _():
-            old_down.start()
-
-        @pl.when(has_up)
-        def _():
-            old_up.start()
 
     def taps_dot(stage, at):
         begin, end = STAGES[stage]
         parts = [
-            ext[kh, pl.ds(kt * clips + at * chunk, chunk)].reshape(chunk * cols, ch)
+            ext[kh, pl.ds(at * chunk, chunk), kt : kt + 2].reshape(places, ch)
             for kt, kh in TAPS[begin:end]
         ]
         return jnp.dot(
@@ -266,6 +262,45 @@
             rows = wbuf.at[pl.ds(i * ch, ch)]
             pltpu.make_async_copy(rows, rows, wsem.at[i]).wait()
 
+    def start(at):
+        conv[at] = taps_dot(0, at)
+
+    weights_here(0)
+    loop(clips // chunk, start)
+
+    @pl.when(s > 0)
+    def _():
+        to_flag.wait_recv()
+        for g in range(halves):
+            to_next[g].wait_recv()
+
+            @pl.when(s > 1)
+            def _():
+                to_after[g].wait_recv()
+
+            for b in range(g * share, (g + 1) * share):
+                both = flag_in[b, 0:1, :] > 1.5
+                first = prev[b, 0].astype(f32)
+                second = prev[b, 1].astype(f32)
+                older = prev2[b].astype(f32)
+                ext[1, b, 1] = jnp.where(both, second, first).astype(bf16)
+                ext[1, b, 0] = jnp.where(both, first, older).astype(bf16)
+
+            @pl.when(has_down)
+            def _():
+                old_down[g].start()
+
+            @pl.when(has_up)
+            def _():
+                old_up[g].start()
+
+    weights_here(1)
+
+    def center(at):
+        conv[at] += taps_dot(1, at)
+
+    loop(clips // chunk, center)
+
     @pl.when(has_up)
     def _():
         own_down.wait_recv()
@@ -274,24 +309,25 @@
     def _():
         own_up.wait_recv()
 
-    weights_here(0)
-    weights_here(1)
-
-    def early(at):
-        conv[at] = taps_dot(0, at) + taps_dot(1, at)
-
-    loop(frames // chunk, early)
     weights_here(2)
 
+    def beside(at):
+        conv[at] += taps_dot(2, at)
+
+    loop(clips // chunk, beside)
+    weights_here(3)
+
     @pl.when(s > 0)
     def _():
-        @pl.when(has_up)
-        def _():
-            old_down.wait_recv()
-
-        @pl.when(has_down)
-        def _():
-            old_up.wait_recv()
+        for g in range(halves):
+
+            @pl.when(has_up)
+            def _():
+                old_down[g].wait_recv()
+
+            @pl.when(has_down)
+            def _():
+                old_up[g].wait_recv()
 
     for copy in small[3:]:
         copy.wait()
@@ -301,27 +337,26 @@
     output_bias = output_bias_ref[...].reshape(1, ch)
 
     def late(at):
-        total = conv[at] + taps_dot(2, at)
-        places = chunk * cols
+        total = conv[at] + taps_dot(3, at)
         column = lax.rem(lax.broadcasted_iota(jnp.int32, (places, ch), 0), cols)
         left = pltpu.roll(total[:, :ch], 1, 0)
         right = pltpu.roll(total[:, 2 * ch :], places - 1, 0)
         summed = total[:, ch : 2 * ch] + jnp.where(column == 0, 0.0, left)
         summed = summed + jnp.where(column == cols - 1, 0.0, right)
         summed = summed + conv_bias
-        at_frames = pl.ds(at * chunk, chunk)
+        at_frames = pl.ds(at * 2 * chunk, 2 * chunk)
         held = residual[at_frames].reshape(places, ch).astype(f32)
         held = (held + summed).astype(bf16)
-        residual[at_frames] = held.reshape(chunk, cols, ch)
+        residual[at_frames] = held.reshape(2 * chunk, cols, ch)
         wide = held.astype(f32)
         mean = jnp.mean(wide * wide, axis=-1, keepdims=True)
         wide = (wide * lax.rsqrt(mean + EPSILON) * attn_gain).astype(bf16)
-        normed[at_frames] = wide.reshape(chunk, cols, ch)
+        normed[at_frames] = wide.reshape(2 * chunk, cols, ch)
 
     for b in range(clips):
         for t in range(2):
-            residual[t * clips + b] = seg_ref[b, t, 0]
-    loop(frames // chunk, late)
+            residual[2 * b + t] = seg_ref[b, t, 0]
+    loop(clips // chunk, late)
 
     there = []
     for k in range(1, n_rows):
@@ -394,7 +429,7 @@
     for b in range(clips):
         count = len_ref[0, b]
         for t in range(2):
-            f = t * clips + b
+            f = 2 * b + t
             live = (count > t).astype(f32)
             summed = residual[f].astype(f32) + returned[f].astype(f32)
             out_ref[b, t, 0] = (summed * live).astype(bf16)
@@ -405,29 +440,31 @@
     @pl.when(s + 1 < n_tm)
     def _():
         to_flag.wait_send()
-        to_next.wait_send()
+        for copy in to_next:
+            copy.wait_send()
 
     @pl.when(s + 2 < n_tm)
     def _():
-        to_after.wait_send()
+        for copy in to_after:
+            copy.wait_send()
 
     @pl.when(has_down)
     def _():
         own_down.wait_send()
 
+        @pl.when(s > 0)
+        def _():
+            for copy in old_down:
+                copy.wait_send()
+
     @pl.when(has_up)
     def _():
         own_up.wait_send()
 
-    @pl.when(s > 0)
-    def _():
-        @pl.when(has_down)
-        def _():
-            old_down.wait_send()
-
-        @pl.when(has_up)
-        def _():
-            old_up.wait_send()
+        @pl.when(s > 0)
+        def _():
+            for copy in old_up:
+                copy.wait_send()
 
 
 def segment(
@@ -448,7 +485,7 @@
     clips, _, _, cols, ch = segment_input.shape
     frames = 2 * clips
     per = frames // n_rows
-    chunk = min(frames, 4)
+    chunk = 2 - clips % 2
     bf16, f32 = jnp.bfloat16, jnp.float32
     vmem = pl.BlockSpec(memory_space=pltpu.VMEM)
     hbm = pl.BlockSpec(memory_space=pl.ANY)
@@ -468,8 +505,8 @@
             pltpu.VMEM((3 * ch,), f32),
             pltpu.VMEM((ch,), f32),
             dma((8,)),
-            pltpu.VMEM((3, 4 * clips, cols, ch), bf16),
-            pltpu.VMEM((2 * clips, cols, ch), bf16),
+            pltpu.VMEM((3, clips, 4, cols, ch), bf16),
+            pltpu.VMEM((clips, 2, cols, ch), bf16),
             pltpu.VMEM((clips, cols, ch), bf16),
             pltpu.VMEM((clips, cols, ch), bf16),
             pltpu.VMEM((clips, 8, ch), f32),
@@ -477,7 +514,7 @@
             pltpu.VMEM((9 * ch, 3 * ch), bf16),
             pltpu.VMEM((ch, 3 * ch), bf16),
             pltpu.VMEM((ch, ch), bf16),
-            pltpu.VMEM((frames // chunk, chunk * cols, 3 * ch), f32),
+            pltpu.VMEM((clips // chunk, 2 * chunk * cols, 3 * ch), f32),
             pltpu.VMEM((frames, cols, ch), bf16),
             pltpu.VMEM((frames, cols, ch), bf16),
             pltpu.VMEM((n_rows, per, cols, ch), bf16),
@@ -487,10 +524,10 @@
             pltpu.VMEM((frames, cols, ch), bf16),
             dma((9,)),
             dma((2,)),
-            dma((4,)),
-            dma((4,)),
-            dma((3,)),
-            dma((3,)),
+            dma((6,)),
+            dma((6,)),
+            dma((5,)),
+            dma((5,)),
             dma((n_rows - 1,)),
             dma((n_rows - 1,)),
             dma((n_rows - 1,)),

time: 24.4 us -> 23.4 us (0.959)
  Pallas kernels: 22.7 us -> 21.7 us
    pallas_call x1, Pallas kernels: 22.7 us -> 21.7 us  [segment(): pl.pallas_call(functools.partial(segment_kernel, n_tm, n_rows, clips, col...]
where the time goes in v3:
time: 23.4 us; the launch traced here: 23.3 us
  Pallas kernels  21.7 us (93%)
  local copies, waits for them, and re-layouts  1.54 us (7%)
    pallas_call x1, Pallas kernels, segment(): pl.pallas_call(functools.partial(segment_kernel, n_tm, n_rows, clips, col...  21.7 us
    unnamed x1, local copies, waits for them, and re-layouts  1.54 us

profile of v3, /device:TPU:2, one launch (start us, length us, event | category | flops | bytes accessed | tf_op | source)
XLA Modules:
  0.0 23.3 jit_solution(9764854667808227002)
XLA Ops:
  0.0 21.7 %segment.1 = bf16[2,2,1,32,384]{4,3,2,1,0:T(8,128)(2,1)} custom-call(bf16[2,2,1,32,384]{4,3,2,1,0:T(8,128)(2,1)} %seg_any.1, bf16[2,2,1,32,384]{4,3,2,1,0:T(8,128)(2,1)} %inner_any.1, s32[1,2]{1,0:T(1,128)} %bitcast.1, f32[384]{0:T(512)} %inner_gain_any.1, bf16[3,3,3,384,384]{4,3,2,1,0:T(8,128)(2,1)} %weight_ref.1, f32[384]{0:T(512)} %conv_bias_any.1, ...), custom_call_target="tpu_custom_call" | custom-call | tf_op jit(solution)/shard_map/segment/pallas_call | solution.py:493
  21.8 1.5 %copy.13 = bf16[2,2,1,32,384]{4,3,2,1,0:T(8,128)(2,1)} copy(bf16[2,2,1,32,384]{4,3,2,1,0:T(8,128)(2,1)} %segment.1) | data formatting | bytes 196608

commit v4 on v3

--- a/solution.py
+++ b/solution.py
@@ -129,17 +129,14 @@
     for copy in small:
         copy.start()
 
-    for i, (kt, kh) in enumerate(TAPS):
-        for kw in range(3):
-            pltpu.make_async_copy(
-                weight_ref.at[kt, kh, kw],
-                wbuf.at[pl.ds(i * ch, ch), pl.ds(kw * ch, ch)],
-                wsem.at[i],
-            ).start()
+    weight_copies = [
+        pltpu.make_async_copy(weight_ref.at[kt, kh], wbuf.at[i], wsem.at[i])
+        for i, (kt, kh) in enumerate(TAPS)
+    ]
     triple_copy = pltpu.make_async_copy(triple_ref, tbuf, psem.at[0])
     output_copy = pltpu.make_async_copy(output_ref, obuf, psem.at[1])
-    triple_copy.start()
-    output_copy.start()
+    for copy in weight_copies[:3]:
+        copy.start()
 
     for copy in small[:3]:
         copy.wait()
@@ -245,22 +242,29 @@
     def _():
         own_up.start()
 
+    for copy in weight_copies[3:]:
+        copy.start()
+    triple_copy.start()
+    output_copy.start()
+
     def taps_dot(stage, at):
         begin, end = STAGES[stage]
         parts = [
             ext[kh, pl.ds(at * chunk, chunk), kt : kt + 2].reshape(places, ch)
             for kt, kh in TAPS[begin:end]
         ]
+        columns = [
+            jnp.concatenate([wbuf[i, kw] for i in range(begin, end)], axis=0) for kw in range(3)
+        ]
         return jnp.dot(
             jnp.concatenate(parts, axis=-1),
-            wbuf[begin * ch : end * ch, :],
+            jnp.concatenate(columns, axis=-1),
             preferred_element_type=f32,
         )
 
     def weights_here(stage):
         for i in range(*STAGES[stage]):
-            rows = wbuf.at[pl.ds(i * ch, ch)]
-            pltpu.make_async_copy(rows, rows, wsem.at[i]).wait()
+            weight_copies[i].wait()
 
     def start(at):
         conv[at] = taps_dot(0, at)
@@ -511,7 +515,7 @@
             pltpu.VMEM((clips, cols, ch), bf16),
             pltpu.VMEM((clips, 8, ch), f32),
             pltpu.VMEM((clips, 8, ch), f32),
-            pltpu.VMEM((9 * ch, 3 * ch), bf16),
+            pltpu.VMEM((9, 3, ch, ch), bf16),
             pltpu.VMEM((ch, 3 * ch), bf16),
             pltpu.VMEM((ch, ch), bf16),
             pltpu.VMEM((clips // chunk, 2 * chunk * cols, 3 * ch), f32),

time: 23.4 us -> 22.8 us (0.974)
  Pallas kernels: 21.7 us -> 21.1 us
    pallas_call x1, Pallas kernels: 21.7 us -> 21.1 us  [segment(): pl.pallas_call(functools.partial(segment_kernel, n_tm, n_rows, clips, col...]
where the time goes in v4:
time: 22.8 us; the launch traced here: 22.7 us
  Pallas kernels  21.1 us (93%)
  local copies, waits for them, and re-layouts  1.54 us (7%)
    pallas_call x1, Pallas kernels, segment(): pl.pallas_call(functools.partial(segment_kernel, n_tm, n_rows, clips, col...  21.1 us
    unnamed x1, local copies, waits for them, and re-layouts  1.54 us

profile of v4, /device:TPU:2, one launch (start us, length us, event | category | flops | bytes accessed | tf_op | source)
XLA Modules:
  0.0 22.7 jit_solution(9718532060770861268)
XLA Ops:
  0.0 21.1 %segment.1 = bf16[2,2,1,32,384]{4,3,2,1,0:T(8,128)(2,1)} custom-call(bf16[2,2,1,32,384]{4,3,2,1,0:T(8,128)(2,1)} %seg_any.1, bf16[2,2,1,32,384]{4,3,2,1,0:T(8,128)(2,1)} %inner_any.1, s32[1,2]{1,0:T(1,128)} %bitcast.1, f32[384]{0:T(512)} %inner_gain_any.1, bf16[3,3,3,384,384]{4,3,2,1,0:T(8,128)(2,1)} %weight_ref.1, f32[384]{0:T(512)} %conv_bias_any.1, ...), custom_call_target="tpu_custom_call" | custom-call | tf_op jit(solution)/shard_map/segment/pallas_call | solution.py:497
  21.1 1.5 %copy.13 = bf16[2,2,1,32,384]{4,3,2,1,0:T(8,128)(2,1)} copy(bf16[2,2,1,32,384]{4,3,2,1,0:T(8,128)(2,1)} %segment.1) | data formatting | bytes 196608

commit v5 on v4

--- a/solution.py
+++ b/solution.py
@@ -87,9 +87,9 @@
     frames = 2 * clips
     per = frames // n_rows
     chunk = 2 - clips % 2
-    places = 2 * chunk * cols
-    halves = 2 if clips % 2 == 0 else 1
+    halves = 2 if clips % 2 == 0 and n_rows % 2 == 0 else 1
     share = clips // halves
+    step = 2 - share % 2
     bf16, f32 = jnp.bfloat16, jnp.float32
 
     barrier = pltpu.get_barrier_semaphore()
@@ -247,10 +247,10 @@
     triple_copy.start()
     output_copy.start()
 
-    def taps_dot(stage, at):
+    def taps_dot(stage, at, chunk):
         begin, end = STAGES[stage]
         parts = [
-            ext[kh, pl.ds(at * chunk, chunk), kt : kt + 2].reshape(places, ch)
+            ext[kh, pl.ds(at * chunk, chunk), kt : kt + 2].reshape(2 * chunk * cols, ch)
             for kt, kh in TAPS[begin:end]
         ]
         columns = [
@@ -267,7 +267,8 @@
             weight_copies[i].wait()
 
     def start(at):
-        conv[at] = taps_dot(0, at)
+        held = taps_dot(0, at, chunk).reshape(chunk, 2 * cols, 3 * ch)
+        conv[pl.ds(at * chunk, chunk)] = held
 
     weights_here(0)
     loop(clips // chunk, start)
@@ -301,7 +302,8 @@
     weights_here(1)
 
     def center(at):
-        conv[at] += taps_dot(1, at)
+        held = taps_dot(1, at, chunk).reshape(chunk, 2 * cols, 3 * ch)
+        conv[pl.ds(at * chunk, chunk)] += held
 
     loop(clips // chunk, center)
 
@@ -316,22 +318,11 @@
     weights_here(2)
 
     def beside(at):
-        conv[at] += taps_dot(2, at)
+        held = taps_dot(2, at, chunk).reshape(chunk, 2 * cols, 3 * ch)
+        conv[pl.ds(at * chunk, chunk)] += held
 
     loop(clips // chunk, beside)
     weights_here(3)
-
-    @pl.when(s > 0)
-    def _():
-        for g in range(halves):
-
-            @pl.when(has_up)
-            def _():
-                old_down[g].wait_recv()
-
-            @pl.when(has_down)
-            def _():
-                old_up[g].wait_recv()
 
     for copy in small[3:]:
         copy.wait()
@@ -341,39 +332,58 @@
     output_bias = output_bias_ref[...].reshape(1, ch)
 
     def late(at):
-        total = conv[at] + taps_dot(3, at)
+        places = 2 * step * cols
+        total = conv[pl.ds(at * step, step)].reshape(places, 3 * ch) + taps_dot(3, at, step)
         column = lax.rem(lax.broadcasted_iota(jnp.int32, (places, ch), 0), cols)
         left = pltpu.roll(total[:, :ch], 1, 0)
         right = pltpu.roll(total[:, 2 * ch :], places - 1, 0)
         summed = total[:, ch : 2 * ch] + jnp.where(column == 0, 0.0, left)
         summed = summed + jnp.where(column == cols - 1, 0.0, right)
         summed = summed + conv_bias
-        at_frames = pl.ds(at * 2 * chunk, 2 * chunk)
+        at_frames = pl.ds(at * 2 * step, 2 * step)
         held = residual[at_frames].reshape(places, ch).astype(f32)
         held = (held + summed).astype(bf16)
-        residual[at_frames] = held.reshape(2 * chunk, cols, ch)
+        residual[at_frames] = held.reshape(2 * step, cols, ch)
         wide = held.astype(f32)
         mean = jnp.mean(wide * wide, axis=-1, keepdims=True)
         wide = (wide * lax.rsqrt(mean + EPSILON) * attn_gain).astype(bf16)
-        normed[at_frames] = wide.reshape(2 * chunk, cols, ch)
+        normed[at_frames] = wide.reshape(2 * step, cols, ch)
 
     for b in range(clips):
         for t in range(2):
             residual[2 * b + t] = seg_ref[b, t, 0]
-    loop(clips // chunk, late)
-
     there = []
     for k in range(1, n_rows):
         peer = lax.rem(r + k, n_rows)
-        copy = remote(
-            normed.at[pl.ds(peer * per, per)],
-            gathered.at[r],
-            to_send.at[k - 1],
-            to_recv.at[k - 1],
-            {"rows": peer},
-        )
-        copy.start()
-        there.append(copy)
+        there.append(
+            remote(
+                normed.at[pl.ds(peer * per, per)],
+                gathered.at[r],
+                to_send.at[k - 1],
+                to_recv.at[k - 1],
+                {"rows": peer},
+            )
+        )
+    for g in range(halves):
+
+        @pl.when(s > 0)
+        def _():
+            @pl.when(has_up)
+            def _():
+                old_down[g].wait_recv()
+
+            @pl.when(has_down)
+            def _():
+                old_up[g].wait_recv()
+
+        first = g * share // step
+        loop(share // step, lambda at: late(first + at))
+        for k in range(1, n_rows):
+
+            @pl.when(lax.rem(r + k, n_rows) // (n_rows // halves) == g)
+            def _():
+                there[k - 1].start()
+
     gathered[r] = normed[pl.ds(r * per, per)]
     triple_copy.wait()
     output_copy.wait()
@@ -489,7 +499,6 @@
     clips, _, _, cols, ch = segment_input.shape
     frames = 2 * clips
     per = frames // n_rows
-    chunk = 2 - clips % 2
     bf16, f32 = jnp.bfloat16, jnp.float32
     vmem = pl.BlockSpec(memory_space=pltpu.VMEM)
     hbm = pl.BlockSpec(memory_space=pl.ANY)
@@ -518,7 +527,7 @@
             pltpu.VMEM((9, 3, ch, ch), bf16),
             pltpu.VMEM((ch, 3 * ch), bf16),
             pltpu.VMEM((ch, ch), bf16),
-            pltpu.VMEM((clips // chunk, 2 * chunk * cols, 3 * ch), f32),
+            pltpu.VMEM((clips, 2 * cols, 3 * ch), f32),
             pltpu.VMEM((frames, cols, ch), bf16),
             pltpu.VMEM((frames, cols, ch), bf16),
             pltpu.VMEM((n_rows, per, cols, ch), bf16),

time: 22.8 us -> 23.1 us (1.013)
  Pallas kernels: 21.1 us -> 21.4 us
    pallas_call x1, Pallas kernels: 21.1 us -> 21.4 us  [segment(): pl.pallas_call(functools.partial(segment_kernel, n_tm, n_rows, clips, col...]
where the time goes in v5:
time: 23.1 us; the launch traced here: 23 us
  Pallas kernels  21.4 us (93%)
  local copies, waits for them, and re-layouts  1.54 us (7%)
    pallas_call x1, Pallas kernels, segment(): pl.pallas_call(functools.partial(segment_kernel, n_tm, n_rows, clips, col...  21.4 us
    unnamed x1, local copies, waits for them, and re-layouts  1.54 us

profile of v5, /device:TPU:2, one launch (start us, length us, event | category | flops | bytes accessed | tf_op | source)
XLA Modules:
  0.0 23.0 jit_solution(5598043215741960635)
XLA Ops:
  0.0 21.4 %segment.1 = bf16[2,2,1,32,384]{4,3,2,1,0:T(8,128)(2,1)} custom-call(bf16[2,2,1,32,384]{4,3,2,1,0:T(8,128)(2,1)} %seg_any.1, bf16[2,2,1,32,384]{4,3,2,1,0:T(8,128)(2,1)} %inner_any.1, s32[1,2]{1,0:T(1,128)} %bitcast.1, f32[384]{0:T(512)} %inner_gain_any.1, bf16[3,3,3,384,384]{4,3,2,1,0:T(8,128)(2,1)} %weight_ref.1, f32[384]{0:T(512)} %conv_bias_any.1, ...), custom_call_target="tpu_custom_call" | custom-call | tf_op jit(solution)/shard_map/segment/pallas_call | solution.py:506
  21.4 1.5 %copy.13 = bf16[2,2,1,32,384]{4,3,2,1,0:T(8,128)(2,1)} copy(bf16[2,2,1,32,384]{4,3,2,1,0:T(8,128)(2,1)} %segment.1) | data formatting | bytes 196608

commit v6 on v5

--- a/solution.py
+++ b/solution.py
@@ -24,7 +24,7 @@
 
 
 TAPS = ((2, 1), (1, 1), (0, 1), (2, 0), (2, 2), (1, 0), (1, 2), (0, 0), (0, 2))
-STAGES = ((0, 1), (1, 3), (3, 5), (5, 9))
+STAGES = ((0, 1), (1, 3), (3, 5), (5, 7), (7, 9))
 
 
 def segment_kernel(
@@ -169,7 +169,7 @@
     @pl.when(s == 0)
     def _():
         ext[1, :, cached] = blank
-        prev[...] = blank
+        prev[...] = jnp.zeros((clips, cols, ch), bf16)
         flag_in[...] = jnp.zeros((clips, 8, ch), f32)
 
         @pl.when(r > 0)
@@ -198,41 +198,29 @@
     has_down, has_up = r < n_rows - 1, r > 0
     own_down = remote(ext.at[1, :, own], ext.at[0, :, own], near_send.at[0], near_recv.at[0], down)
     own_up = remote(ext.at[1, :, own], ext.at[2, :, own], near_send.at[1], near_recv.at[1], up)
-    to_flag = remote(flag_out, flag_in, tm_send.at[0], tm_recv.at[0], {"tm": s + 1})
-    old_down, old_up, to_next, to_after = [], [], [], []
-    for g in range(halves):
-        part = pl.ds(g * share, share)
-        mine = ext.at[1, part, cached]
-        i, j = 2 + 2 * g, 3 + 2 * g
-        old_down.append(
-            remote(mine, ext.at[0, part, cached], near_send.at[i], near_recv.at[i], down)
-        )
-        old_up.append(remote(mine, ext.at[2, part, cached], near_send.at[j], near_recv.at[j], up))
-        i, j = 1 + 2 * g, 2 + 2 * g
-        to_next.append(
-            remote(
-                ext.at[1, part, own], prev.at[part], tm_send.at[i], tm_recv.at[i], {"tm": s + 1}
-            )
-        )
-        to_after.append(
-            remote(last.at[part], prev2.at[part], tm_send.at[j], tm_recv.at[j], {"tm": s + 2})
-        )
+    old_down, old_up = [], []
+    for slot in range(2):
+        mine = ext.at[1, :, slot]
+        i, j = 2 + 2 * slot, 3 + 2 * slot
+        old_down.append(remote(mine, ext.at[0, :, slot], near_send.at[i], near_recv.at[i], down))
+        old_up.append(remote(mine, ext.at[2, :, slot], near_send.at[j], near_recv.at[j], up))
+    after, later = {"tm": s + 1}, {"tm": s + 2}
+    to_flag = remote(flag_out, flag_in, tm_send.at[0], tm_recv.at[0], after)
+    to_last = remote(last, ext.at[1, :, 1], tm_send.at[1], tm_recv.at[1], after)
+    to_first = remote(ext.at[1, :, 2], prev, tm_send.at[2], tm_recv.at[2], after)
+    to_after = remote(last, prev2, tm_send.at[3], tm_recv.at[3], later)
 
     pl.semaphore_wait(barrier, expected)
 
     @pl.when(s + 1 < n_tm)
     def _():
+        to_last.start()
         to_flag.start()
-
-    for g in range(halves):
-
-        @pl.when(s + 1 < n_tm)
-        def _():
-            to_next[g].start()
-
-        @pl.when(s + 2 < n_tm)
-        def _():
-            to_after[g].start()
+        to_first.start()
+
+    @pl.when(s + 2 < n_tm)
+    def _():
+        to_after.start()
 
     @pl.when(has_down)
     def _():
@@ -273,31 +261,42 @@
     weights_here(0)
     loop(clips // chunk, start)
 
-    @pl.when(s > 0)
-    def _():
-        to_flag.wait_recv()
-        for g in range(halves):
-            to_next[g].wait_recv()
-
-            @pl.when(s > 1)
+    def pass_on(slot):
+        @pl.when(has_down)
+        def _():
+            old_down[slot].start()
+
+        @pl.when(has_up)
+        def _():
+            old_up[slot].start()
+
+    def passed_on(slot):
+        @pl.when(s > 0)
+        def _():
+            @pl.when(has_up)
             def _():
-                to_after[g].wait_recv()
-
-            for b in range(g * share, (g + 1) * share):
-                both = flag_in[b, 0:1, :] > 1.5
-                first = prev[b, 0].astype(f32)
-                second = prev[b, 1].astype(f32)
-                older = prev2[b].astype(f32)
-                ext[1, b, 1] = jnp.where(both, second, first).astype(bf16)
-                ext[1, b, 0] = jnp.where(both, first, older).astype(bf16)
+                old_down[slot].wait_recv()
 
             @pl.when(has_down)
             def _():
-                old_down[g].start()
-
-            @pl.when(has_up)
-            def _():
-                old_up[g].start()
+                old_up[slot].wait_recv()
+
+    @pl.when(s > 0)
+    def _():
+        to_last.wait_recv()
+        pass_on(1)
+        to_flag.wait_recv()
+        to_first.wait_recv()
+
+        @pl.when(s > 1)
+        def _():
+            to_after.wait_recv()
+
+        for b in range(clips):
+            both = flag_in[b, 0:1, :] > 1.5
+            older = jnp.where(both, prev[b].astype(f32), prev2[b].astype(f32))
+            ext[1, b, 0] = older.astype(bf16)
+        pass_on(0)
 
     weights_here(1)
 
@@ -323,6 +322,15 @@
 
     loop(clips // chunk, beside)
     weights_here(3)
+    passed_on(1)
+
+    def nearer(at):
+        held = taps_dot(3, at, chunk).reshape(chunk, 2 * cols, 3 * ch)
+        conv[pl.ds(at * chunk, chunk)] += held
+
+    loop(clips // chunk, nearer)
+    weights_here(4)
+    passed_on(0)
 
     for copy in small[3:]:
         copy.wait()
@@ -333,7 +341,7 @@
 
     def late(at):
         places = 2 * step * cols
-        total = conv[pl.ds(at * step, step)].reshape(places, 3 * ch) + taps_dot(3, at, step)
+        total = conv[pl.ds(at * step, step)].reshape(places, 3 * ch) + taps_dot(4, at, step)
         column = lax.rem(lax.broadcasted_iota(jnp.int32, (places, ch), 0), cols)
         left = pltpu.roll(total[:, :ch], 1, 0)
         right = pltpu.roll(total[:, 2 * ch :], places - 1, 0)
@@ -365,17 +373,6 @@
             )
         )
     for g in range(halves):
-
-        @pl.when(s > 0)
-        def _():
-            @pl.when(has_up)
-            def _():
-                old_down[g].wait_recv()
-
-            @pl.when(has_down)
-            def _():
-                old_up[g].wait_recv()
-
         first = g * share // step
         loop(share // step, lambda at: late(first + at))
         for k in range(1, n_rows):
@@ -454,13 +451,12 @@
     @pl.when(s + 1 < n_tm)
     def _():
         to_flag.wait_send()
-        for copy in to_next:
-            copy.wait_send()
+        to_last.wait_send()
+        to_first.wait_send()
 
     @pl.when(s + 2 < n_tm)
     def _():
-        for copy in to_after:
-            copy.wait_send()
+        to_after.wait_send()
 
     @pl.when(has_down)
     def _():
@@ -519,7 +515,7 @@
             pltpu.VMEM((ch,), f32),
             dma((8,)),
             pltpu.VMEM((3, clips, 4, cols, ch), bf16),
-            pltpu.VMEM((clips, 2, cols, ch), bf16),
+            pltpu.VMEM((clips, cols, ch), bf16),
             pltpu.VMEM((clips, cols, ch), bf16),
             pltpu.VMEM((clips, cols, ch), bf16),
             pltpu.VMEM((clips, 8, ch), f32),
@@ -539,8 +535,8 @@
             dma((2,)),
             dma((6,)),
             dma((6,)),
-            dma((5,)),
-            dma((5,)),
+            dma((4,)),
+            dma((4,)),
             dma((n_rows - 1,)),
             dma((n_rows - 1,)),
             dma((n_rows - 1,)),

time: 23.1 us -> 22.9 us (level)
  no operation moved by 1% of the time
where the time goes in v6:
time: 22.9 us; the launch traced here: 22.8 us
  Pallas kernels  21.2 us (93%)
  local copies, waits for them, and re-layouts  1.54 us (7%)
    pallas_call x1, Pallas kernels, segment(): pl.pallas_call(functools.partial(segment_kernel, n_tm, n_rows, clips, col...  21.2 us
    unnamed x1, local copies, waits for them, and re-layouts  1.54 us

profile of v6, /device:TPU:2, one launch (start us, length us, event | category | flops | bytes accessed | tf_op | source)
XLA Modules:
  0.0 22.8 jit_solution(7991997631300985120)
XLA Ops:
  0.0 21.2 %segment.1 = bf16[2,2,1,32,384]{4,3,2,1,0:T(8,128)(2,1)} custom-call(bf16[2,2,1,32,384]{4,3,2,1,0:T(8,128)(2,1)} %seg_any.1, bf16[2,2,1,32,384]{4,3,2,1,0:T(8,128)(2,1)} %inner_any.1, s32[1,2]{1,0:T(1,128)} %bitcast.1, f32[384]{0:T(512)} %inner_gain_any.1, bf16[3,3,3,384,384]{4,3,2,1,0:T(8,128)(2,1)} %weight_ref.1, f32[384]{0:T(512)} %conv_bias_any.1, ...), custom_call_target="tpu_custom_call" | custom-call | tf_op jit(solution)/shard_map/segment/pallas_call | solution.py:502
  21.2 1.5 %copy.13 = bf16[2,2,1,32,384]{4,3,2,1,0:T(8,128)(2,1)} copy(bf16[2,2,1,32,384]{4,3,2,1,0:T(8,128)(2,1)} %segment.1) | data formatting | bytes 196608

commit v7 on v6

--- a/solution.py
+++ b/solution.py
@@ -67,6 +67,7 @@
     residual,
     normed,
     gathered,
+    qbuf,
     kbuf,
     vbuf,
     result,
@@ -135,8 +136,8 @@
     ]
     triple_copy = pltpu.make_async_copy(triple_ref, tbuf, psem.at[0])
     output_copy = pltpu.make_async_copy(output_ref, obuf, psem.at[1])
-    for copy in weight_copies[:3]:
-        copy.start()
+    for copy in weight_copies + [triple_copy, output_copy]:
+        copy.start(priority=1)
 
     for copy in small[:3]:
         copy.wait()
@@ -230,10 +231,6 @@
     def _():
         own_up.start()
 
-    for copy in weight_copies[3:]:
-        copy.start()
-    triple_copy.start()
-    output_copy.start()
 
     def taps_dot(stage, at, chunk):
         begin, end = STAGES[stage]
@@ -387,23 +384,35 @@
     for copy in there:
         copy.wait_recv()
 
-    groups = max(1, n_rows * cols // 128)
-    height = n_rows // groups
+    block = n_rows if n_rows % 4 else 4
+    group = n_rows if n_rows % 2 else 2 if n_rows == 4 else block
+    turns = n_rows // group
+    back = []
+    for k in range(1, n_rows):
+        peer = lax.rem(r + k, n_rows)
+        back.append(
+            remote(
+                result.at[peer],
+                returned.at[pl.ds(r * per, per)],
+                back_send.at[k - 1],
+                back_recv.at[k - 1],
+                {"rows": peer},
+            )
+        )
 
     for frame in range(per):
 
         def project(at):
-            x = gathered[pl.ds(at * height, height), frame].reshape(height * cols, ch)
-            packed = jnp.dot(x, tbuf[:, ch:], preferred_element_type=f32)
-            packed = packed + triple_bias[:, ch:]
-            rows = pl.ds(at * height * cols, height * cols)
-            kbuf[rows] = packed[:, :ch]
-            vbuf[rows] = packed[:, ch:].astype(bf16)
-
-        def attend_rows(at):
-            x = gathered[pl.ds(at * height, height), frame].reshape(height * cols, ch)
-            queries = jnp.dot(x, tbuf[:, :ch], preferred_element_type=f32)
-            queries = queries + triple_bias[:, :ch]
+            x = gathered[pl.ds(at * block, block), frame].reshape(block * cols, ch)
+            packed = jnp.dot(x, tbuf[...], preferred_element_type=f32) + triple_bias
+            rows = pl.ds(at * block * cols, block * cols)
+            qbuf[rows] = packed[:, :ch]
+            kbuf[rows] = packed[:, ch : 2 * ch]
+            vbuf[rows] = packed[:, 2 * ch :].astype(bf16)
+
+        def attend_rows(turn):
+            at = lax.rem(r // group + turns // 2 + turn, turns)
+            queries = qbuf[pl.ds(at * group * cols, group * cols)]
             scores = lax.dot_general(
                 queries,
                 kbuf[...],
@@ -416,23 +425,21 @@
             attended = jnp.dot(weights, vbuf[...], preferred_element_type=f32).astype(bf16)
             projected = jnp.dot(attended, obuf[...], preferred_element_type=f32)
             projected = (projected + output_bias).astype(bf16)
-            result[pl.ds(at * height, height), frame] = projected.reshape(height, cols, ch)
-
-        loop(groups, project)
-        loop(groups, attend_rows)
-
-    back = []
-    for k in range(1, n_rows):
-        peer = lax.rem(r + k, n_rows)
-        copy = remote(
-            result.at[peer],
-            returned.at[pl.ds(r * per, per)],
-            back_send.at[k - 1],
-            back_recv.at[k - 1],
-            {"rows": peer},
-        )
-        copy.start()
-        back.append(copy)
+            result[pl.ds(at * group, group), frame] = projected.reshape(group, cols, ch)
+            if frame == per - 1:
+                for k in range(1, n_rows):
+
+                    @pl.when(lax.rem(r + k, n_rows) // group == at)
+                    def _():
+                        back[k - 1].start()
+
+        loop(n_rows // block, project)
+        if turns <= 2:
+            for turn in range(turns):
+                attend_rows(turn)
+        else:
+            loop(turns, attend_rows)
+
     returned[pl.ds(r * per, per)] = result[r]
     for copy in back:
         copy.wait_recv()
@@ -528,6 +535,7 @@
             pltpu.VMEM((frames, cols, ch), bf16),
             pltpu.VMEM((n_rows, per, cols, ch), bf16),
             pltpu.VMEM((n_rows * cols, ch), f32),
+            pltpu.VMEM((n_rows * cols, ch), f32),
             pltpu.VMEM((n_rows * cols, ch), bf16),
             pltpu.VMEM((n_rows, per, cols, ch), bf16),
             pltpu.VMEM((frames, cols, ch), bf16),

time: 22.9 us -> 22.9 us (level)
  no operation moved by 1% of the time
where the time goes in v7:
time: 22.9 us; the launch traced here: 22.7 us
  Pallas kernels  21.2 us (93%)
  local copies, waits for them, and re-layouts  1.54 us (7%)
    pallas_call x1, Pallas kernels, segment(): pl.pallas_call(functools.partial(segment_kernel, n_tm, n_rows, clips, col...  21.2 us
    unnamed x1, local copies, waits for them, and re-layouts  1.54 us

profile of v7, /device:TPU:2, one launch (start us, length us, event | category | flops | bytes accessed | tf_op | source)
XLA Modules:
  0.0 22.7 jit_solution(8710300737756622534)
XLA Ops:
  0.0 21.2 %segment.1 = bf16[2,2,1,32,384]{4,3,2,1,0:T(8,128)(2,1)} custom-call(bf16[2,2,1,32,384]{4,3,2,1,0:T(8,128)(2,1)} %seg_any.1, bf16[2,2,1,32,384]{4,3,2,1,0:T(8,128)(2,1)} %inner_any.1, s32[1,2]{1,0:T(1,128)} %bitcast.1, f32[384]{0:T(512)} %inner_gain_any.1, bf16[3,3,3,384,384]{4,3,2,1,0:T(8,128)(2,1)} %weight_ref.1, f32[384]{0:T(512)} %conv_bias_any.1, ...), custom_call_target="tpu_custom_call" | custom-call | tf_op jit(solution)/shard_map/segment/pallas_call | solution.py:509
  21.2 1.5 %copy.13 = bf16[2,2,1,32,384]{4,3,2,1,0:T(8,128)(2,1)} copy(bf16[2,2,1,32,384]{4,3,2,1,0:T(8,128)(2,1)} %segment.1) | data formatting | bytes 196608

commit v8 on v7

--- a/solution.py
+++ b/solution.py
@@ -508,7 +508,7 @@
     dma = pltpu.SemaphoreType.DMA
     return pl.pallas_call(
         functools.partial(segment_kernel, n_tm, n_rows, clips, cols, ch),
-        out_shape=jax.ShapeDtypeStruct(segment_input.shape, bf16),
+        out_shape=pltpu.VMEM(segment_input.shape, bf16),
         in_specs=[hbm] * 11,
         out_specs=vmem,
         scratch_shapes=[

time: 22.9 us -> 21.4 us (0.934)
  local copies, waits for them, and re-layouts: 1.54 us -> 0.64 us
  Pallas kernels: 21.2 us -> 20.6 us
    unnamed x1, local copies, waits for them, and re-layouts: 1.54 us -> 0.64 us
    pallas_call x1, Pallas kernels: 21.2 us -> 20.6 us  [segment(): pl.pallas_call(functools.partial(segment_kernel, n_tm, n_rows, clips, col...]
where the time goes in v8:
time: 21.4 us; the launch traced here: 21.2 us
  Pallas kernels  20.6 us (96%)
  local copies, waits for them, and re-layouts  0.64 us (3%)
    pallas_call x1, Pallas kernels, segment(): pl.pallas_call(functools.partial(segment_kernel, n_tm, n_rows, clips, col...  20.6 us
    unnamed x1, local copies, waits for them, and re-layouts  0.64 us

profile of v8, /device:TPU:2, one launch (start us, length us, event | category | flops | bytes accessed | tf_op | source)
XLA Modules:
  0.0 21.2 jit_solution(13721029845077841744)
XLA Ops:
  0.0 20.6 %segment.1 = bf16[2,2,1,32,384]{4,3,2,1,0:T(8,128)(2,1)S(1)} custom-call(bf16[2,2,1,32,384]{4,3,2,1,0:T(8,128)(2,1)} %seg_any.1, bf16[2,2,1,32,384]{4,3,2,1,0:T(8,128)(2,1)} %inner_any.1, s32[1,2]{1,0:T(1,128)} %bitcast.1, f32[384]{0:T(512)} %inner_gain_any.1, bf16[3,3,3,384,384]{4,3,2,1,0:T(8,128)(2,1)} %weight_ref.1, f32[384]{0:T(512)} %conv_bias_any.1, ...), custom_call_target="tpu_custom_call" | custom-call | tf_op jit(solution)/shard_map/segment/pallas_call | solution.py:509
  20.6 0.6 %copy.13 = bf16[2,2,1,32,384]{4,3,2,1,0:T(8,128)(2,1)} copy(bf16[2,2,1,32,384]{4,3,2,1,0:T(8,128)(2,1)S(1)} %segment.1) | data formatting | bytes 196608

commit v9 on v8

--- a/solution.py
+++ b/solution.py
@@ -21,6 +21,13 @@
             return carry
 
         lax.fori_loop(0, count, one, 0)
+
+
+def in_three(x):
+    high = x.astype(jnp.bfloat16)
+    rest = x - high.astype(jnp.float32)
+    middle = rest.astype(jnp.bfloat16)
+    return high, middle, (rest - middle.astype(jnp.float32)).astype(jnp.bfloat16)
 
 
 TAPS = ((2, 1), (1, 1), (0, 1), (2, 0), (2, 2), (1, 0), (1, 2), (0, 0), (0, 2))
@@ -406,19 +413,17 @@
             x = gathered[pl.ds(at * block, block), frame].reshape(block * cols, ch)
             packed = jnp.dot(x, tbuf[...], preferred_element_type=f32) + triple_bias
             rows = pl.ds(at * block * cols, block * cols)
-            qbuf[rows] = packed[:, :ch]
-            kbuf[rows] = packed[:, ch : 2 * ch]
+            high, middle, low = in_three(packed[:, :ch])
+            qbuf[rows] = jnp.concatenate([high, high, middle, high, middle, low], axis=-1)
+            high, middle, low = in_three(packed[:, ch : 2 * ch])
+            kbuf[rows] = jnp.concatenate([high, middle, high, low, middle, high], axis=-1)
             vbuf[rows] = packed[:, 2 * ch :].astype(bf16)
 
         def attend_rows(turn):
             at = lax.rem(r // group + turns // 2 + turn, turns)
             queries = qbuf[pl.ds(at * group * cols, group * cols)]
             scores = lax.dot_general(
-                queries,
-                kbuf[...],
-                (((1,), (1,)), ((), ())),
-                precision=lax.Precision.HIGHEST,
-                preferred_element_type=f32,
+                queries, kbuf[...], (((1,), (1,)), ((), ())), preferred_element_type=f32
             ) / math.sqrt(ch)
             exponent = jnp.exp(scores - jnp.max(scores, axis=-1, keepdims=True))
             weights = (exponent / jnp.sum(exponent, axis=-1, keepdims=True)).astype(bf16)
@@ -534,8 +539,8 @@
             pltpu.VMEM((frames, cols, ch), bf16),
             pltpu.VMEM((frames, cols, ch), bf16),
             pltpu.VMEM((n_rows, per, cols, ch), bf16),
-            pltpu.VMEM((n_rows * cols, ch), f32),
-            pltpu.VMEM((n_rows * cols, ch), f32),
+            pltpu.VMEM((n_rows * cols, 6 * ch), bf16),
+            pltpu.VMEM((n_rows * cols, 6 * ch), bf16),
             pltpu.VMEM((n_rows * cols, ch), bf16),
             pltpu.VMEM((n_rows, per, cols, ch), bf16),
             pltpu.VMEM((frames, cols, ch), bf16),

time: 21.4 us -> 21.5 us (level)
  no operation moved by 1% of the time
where the time goes in v9:
time: 21.5 us; the launch traced here: 21.3 us
  Pallas kernels  20.7 us (96%)
  local copies, waits for them, and re-layouts  0.64 us (3%)
    pallas_call x1, Pallas kernels, segment(): pl.pallas_call(functools.partial(segment_kernel, n_tm, n_rows, clips, col...  20.7 us
    unnamed x1, local copies, waits for them, and re-layouts  0.64 us

profile of v9, /device:TPU:2, one launch (start us, length us, event | category | flops | bytes accessed | tf_op | source)
XLA Modules:
  0.0 21.3 jit_solution(7874710232655401514)
XLA Ops:
  0.0 20.7 %segment.1 = bf16[2,2,1,32,384]{4,3,2,1,0:T(8,128)(2,1)S(1)} custom-call(bf16[2,2,1,32,384]{4,3,2,1,0:T(8,128)(2,1)} %seg_any.1, bf16[2,2,1,32,384]{4,3,2,1,0:T(8,128)(2,1)} %inner_any.1, s32[1,2]{1,0:T(1,128)} %bitcast.1, f32[384]{0:T(512)} %inner_gain_any.1, bf16[3,3,3,384,384]{4,3,2,1,0:T(8,128)(2,1)} %weight_ref.1, f32[384]{0:T(512)} %conv_bias_any.1, ...), custom_call_target="tpu_custom_call" | custom-call | tf_op jit(solution)/shard_map/segment/pallas_call | solution.py:514
  20.7 0.6 %copy.13 = bf16[2,2,1,32,384]{4,3,2,1,0:T(8,128)(2,1)} copy(bf16[2,2,1,32,384]{4,3,2,1,0:T(8,128)(2,1)S(1)} %segment.1) | data formatting | bytes 196608
